TPU v7x, 128 devices: a whole 4x4x4 slice. The times are simulated.
128 devices in a mesh: blk: 16 (over x_hi, z, core), group: 8 (over y, x_lo).
Axes of the slice: x: 4 (x_hi: 2, x_lo: 2; x = x_hi * 2 + x_lo), y: 4, z: 4, core: 2. Of those that a mesh axis runs over, the one named last changes fastest.
Arguments:
- queries: bfloat16 [65536, 4096], P(('blk', 'group'))
- passages: bfloat16 [8192, 4096], P(('blk', 'group'))
- positives: int32 [65536], P(('blk', 'group')), may hold values from 0 to 1023
- hard_ids: int32 [65536, 8], P(('blk', 'group')), may hold values from 0 to 8191, as said below
Outputs:
- query_grads: bfloat16 [65536, 4096], P(('blk', 'group'))
- passage_grads: bfloat16 [8192, 4096], P(('blk', 'group'))
- losses: float32 [65536], P(('blk', 'group'))
Inputs may be any that keep to these rules, and one draw needn't show every extreme that they name: `hard_ids`: ids are passage rows. The 8 ids of a query are distinct. Among the queries of one aligned block of 512 query rows, at most 4 distinct ids fall in any aligned block of 64 passage rows, and exactly 4 in some such block.
All inputs are finite; a program needn't handle non-finite values.
Results may differ from a plain program's by a relative error of at most 0.02.
Values may be sent and summed in bfloat16 or wider, within the bound.
A program may use at most 128 MiB of HBM per device.

v0:
```python
import jax
import jax.numpy as jnp
from jax import lax
from jax.sharding import PartitionSpec as P

CAP = 4


logit_scale = 20.0
tiny_eps = 1e-06


def unit_rows(matrix):
    values = matrix.astype(jnp.float32)
    norms = jnp.sqrt(jnp.sum(values * values, axis=-1, keepdims=True) + tiny_eps)
    return (values / norms, norms)


def contract_rows(left, right):
    return lax.dot_general(
        left, right, (((1,), (1,)), ((), ())), preferred_element_type=jnp.float32
    )


def contract_cols(left, right):
    return lax.dot_general(
        left, right, (((0,), (0,)), ((), ())), preferred_element_type=jnp.float32
    )


def shards(queries, passages, positives, hard_ids):
    blocks = lax.axis_size("blk")
    groups = lax.axis_size("group")
    peers = blocks * groups
    query_count, feature_dim = queries.shape
    passage_count = passages.shape[0]
    query_unit, query_norm = unit_rows(queries)
    query_hat = query_unit.astype(jnp.bfloat16)
    owners = hard_ids // passage_count
    flat_ids = hard_ids.reshape(-1)
    wanted = (
        jnp.zeros((peers * passage_count,), jnp.int32)
        .at[flat_ids]
        .max(1)
        .reshape(peers, passage_count)
    )
    ranked = jnp.cumsum(wanted, axis=1) - wanted
    chosen = (wanted[:, :, None] == 1) & (
        ranked[:, :, None] == jnp.arange(CAP, dtype=jnp.int32)[None, None, :]
    )
    local_table = jnp.sum(
        jnp.where(chosen, jnp.arange(passage_count, dtype=jnp.int32)[None, :, None], 0), axis=1
    )
    slot_index = owners * CAP + ranked.reshape(-1)[flat_ids].reshape(owners.shape)
    requested = lax.all_to_all(
        local_table, ("blk", "group"), split_axis=0, concat_axis=0, tiled=True
    )
    outgoing = passages[requested.reshape(-1)].reshape(peers, CAP, feature_dim)
    fetched = lax.all_to_all(
        outgoing, ("blk", "group"), split_axis=0, concat_axis=0, tiled=True
    ).reshape(peers * CAP, feature_dim)
    fetched_hat = unit_rows(fetched)[0].astype(jnp.bfloat16)
    slot_scores = logit_scale * contract_rows(query_hat, fetched_hat)
    hard_scores = jnp.take_along_axis(slot_scores, slot_index, axis=1)
    gathered = lax.all_gather(passages, "blk", axis=0, tiled=True)
    cycle_hat = unit_rows(gathered)[0].astype(jnp.bfloat16)
    cycle_scores = logit_scale * contract_rows(query_hat, cycle_hat)
    cycle_total = jnp.sum(jnp.exp(cycle_scores), axis=1)
    cycle_lse = jnp.log(cycle_total)
    positive_score = jnp.take_along_axis(cycle_scores, positives[:, None], axis=1)[:, 0]
    hard_lse = jnp.log(jnp.exp(positive_score) + jnp.sum(jnp.exp(hard_scores), axis=1))
    losses = cycle_lse + hard_lse - 2.0 * positive_score
    positive_weight = jnp.exp(positive_score - hard_lse)
    hard_weight = jnp.exp(hard_scores - hard_lse[:, None]).astype(jnp.bfloat16)
    onehot = jnp.arange(cycle_scores.shape[1], dtype=jnp.int32)[None, :] == positives[:, None]
    cycle_weight = (
        jnp.exp(cycle_scores - cycle_lse[:, None])
        - jnp.where(onehot, (2.0 - positive_weight)[:, None], 0.0)
    ).astype(jnp.bfloat16)
    slot_match = slot_index[:, :, None] == jnp.arange(peers * CAP, dtype=jnp.int32)[None, None, :]
    weight_table = jnp.sum(
        jnp.where(slot_match, hard_weight.astype(jnp.float32)[:, :, None], 0.0), axis=1
    ).astype(jnp.bfloat16)
    query_sum = logit_scale * (
        jnp.dot(cycle_weight, cycle_hat, preferred_element_type=jnp.float32)
        + jnp.dot(weight_table, fetched_hat, preferred_element_type=jnp.float32)
    )
    query_grads = (
        (query_sum - query_unit * jnp.sum(query_unit * query_sum, axis=1, keepdims=True))
        / query_norm
    ).astype(jnp.bfloat16)
    cycle_sum = lax.psum_scatter(
        (logit_scale * contract_cols(cycle_weight, query_hat)).astype(jnp.bfloat16),
        "blk",
        scatter_dimension=0,
        tiled=True,
    ).astype(jnp.float32)
    slot_sums = (
        (logit_scale * contract_cols(weight_table, query_hat))
        .astype(jnp.bfloat16)
        .reshape(peers, CAP, feature_dim)
    )
    returned = lax.all_to_all(
        slot_sums, ("blk", "group"), split_axis=0, concat_axis=0, tiled=True
    ).reshape(peers * CAP, feature_dim)
    placement = (
        jnp.arange(passage_count, dtype=jnp.int32)[:, None] == requested.reshape(-1)[None, :]
    ).astype(jnp.bfloat16)
    hard_sum = jnp.dot(placement, returned, preferred_element_type=jnp.float32)
    passage_sum = cycle_sum + hard_sum
    passage_unit, passage_norm = unit_rows(passages)
    passage_grads = (
        (passage_sum - passage_unit * jnp.sum(passage_unit * passage_sum, axis=1, keepdims=True))
        / passage_norm
    ).astype(jnp.bfloat16)
    return (query_grads, passage_grads, losses)


def solution(mesh):
    in_specs = (
        P(("blk", "group"), None),
        P(("blk", "group"), None),
        P(("blk", "group")),
        P(("blk", "group"), None),
    )
    out_specs = (P(("blk", "group"), None), P(("blk", "group"), None), P(("blk", "group")))
    return jax.shard_map(shards, mesh=mesh, in_specs=in_specs, out_specs=out_specs, check_vma=False)
```

profile of v0, /device:TPU:1, one launch (start us, length us, event | category | flops | bytes accessed | tf_op | source)
XLA Modules:
  0.0 359.7 jit_solution(17857323990208603848)
XLA Ops:
  7.2 0.0 all-gather.2.cloned.1.call-start
  7.2 0.7 all-gather.2.cloned.1.call-update
  7.9 0.8 copy.39
  8.8 0.2 reshape.192
  9.0 22.4 %scatter_custom_fusion = s32[8192]{0:T(1024)S(1)} fusion(s32[4096]{0:T(1024)S(1)} %bitcast.21, s32[4096]{0:T(1024)S(1)} %broadcast.146, s32[]{:T(128)} %constant.29.clone.1), kind=kCustom, calls=%fused_computation.53 | custom fusion | flops 4096 | bytes 32772 | tf_op jit(solution)/shard_map/scatter-max | solution.py:44
  31.4 0.1 reshape.193
  31.5 0.1 copy.40
  31.5 0.1 reduce_window_sum.13
  31.7 0.1 copy.43
  31.8 0.1 copy.45
  31.9 20.8 %all_to_all.19 = s32[128,1,4]{2,1,0:T(1,128)S(1)} all-to-all(s32[128,1,4]{2,1,0:T(1,128)S(1)} %copy.45), channel_id=1, replica_groups=mesh['blk'=16,'group'=8] {'blk','group'}, dimensions={0} | all-to-all | bytes 4096 | tf_op jit(solution)/shard_map/all_to_all | solution.py:55
  52.7 0.5 broadcast.191
  53.2 0.8 reduce.6
  54.0 0.1 reshape.195
  54.2 4.4 %gather_fusion.1 = bf16[512,4096]{1,0:T(8,128)(2,1)} fusion(bf16[64,4096]{1,0:T(8,128)(2,1)S(1)} %copy-done, s32[1024]{0:T(1024)S(1)} %pad_clamp_fusion), kind=kCustom, calls=%fused_computation.1 | custom fusion | bytes 8390656 | tf_op jit(solution)/shard_map/gather | solution.py:58
  58.6 7.2 %reshape.196 = bf16[128,4,4096]{2,1,0:T(4,128)(2,1)} reshape(bf16[512,4096]{1,0:T(8,128)(2,1)} %gather_fusion.1) | data formatting | bytes 8388608 | tf_op jit(solution)/shard_map/reshape | solution.py:58
  65.8 5.6 %all-to-all-start.1 = ((bf16[128,4,4096]{2,1,0:T(4,128)(2,1)}), bf16[128,4,4096]{2,1,0:T(4,128)(2,1)}, u32[]{:S(2)}, u32[]{:S(2)}) async-start(bf16[128,4,4096]{2,1,0:T(4,128)(2,1)} %reshape.196), calls=%async_computation.1 | async-start | bytes 8388608 | tf_op jit(solution)/shard_map/all_to_all | solution.py:59
  71.4 0.2 reduce-scatter.2.cloned.1.call-start
  71.7 0.1 copy.41
  71.8 0.1 reduce_window_sum.14
  71.9 0.0 copy-start.9
  71.9 23.0 %gather_fusion = s32[4096]{0:T(1024)S(1)} fusion(s32[8192]{0:T(1024)S(1)} %sub.55, s32[4096]{0:T(1024)S(1)} %broadcast_clamp_fusion), kind=kCustom, calls=%fused_computation | custom fusion | bytes 49152 | tf_op jit(solution)/shard_map/gather | solution.py:54
  94.9 0.2 reshape.194
  95.1 0.1 copy.42
  95.2 0.1 copy.46
  95.4 0.2 reshape.225
  95.6 3.1 fusion.2
  98.7 25.4 %all-to-all-done.1 = bf16[128,4,4096]{2,1,0:T(4,128)(2,1)} async-done(((bf16[128,4,4096]{2,1,0:T(4,128)(2,1)}), bf16[128,4,4096]{2,1,0:T(4,128)(2,1)}, u32[]{:S(2)}, u32[]{:S(2)}) %all-to-all-start.1) | async-done | bytes 4194336 | tf_op jit(solution)/shard_map/all_to_all | solution.py:59
  124.1 4.6 %multiply_reduce_fusion.1 = f32[128,4]{1,0:T(8,128)S(1)} fusion(bf16[128,4,4096]{2,1,0:T(4,128)(2,1)} %all-to-all-done.1), kind=kLoop, calls=%fused_computation.20 | loop fusion | flops 6290944 | bytes 4196352 | tf_op jit(solution)/shard_map/reduce_sum | solution.py:15
  128.7 0.1 sqrt.38
  128.8 7.4 %reshape.200 = f32[512,4096]{1,0:T(8,128)} reshape(bf16[128,4,4096]{2,1,0:T(4,128)(2,1)} %all-to-all-done.1) | data formatting | bytes 12582912 | tf_op jit(solution)/shard_map/convert_element_type | solution.py:14
  136.2 4.8 %divide_convert_fusion.1 = bf16[512,4096]{1,0:T(8,128)(2,1)S(1)} fusion(f32[512,4096]{1,0:T(8,128)} %reshape.200, f32[512]{0:T(512)S(1)} %sqrt.38), kind=kLoop, calls=%fused_computation.19 | loop fusion | flops 4194304 | bytes 12584960 | tf_op jit(solution)/shard_map/convert_element_type | solution.py:62
  141.0 2.0 copy-done.3
  143.0 2.4 convolution_multiply_fusion.1
  145.4 33.0 %gather_fusion.3 = f32[4096]{0:T(1024)S(1)} fusion(f32[512,512]{1,0:T(8,128)S(1)} %convolution_multiply_fusion.1, s32[4096]{0:T(1024)S(1)} %reshape.225), kind=kCustom, calls=%fused_computation.3 | custom fusion | bytes 65536 | tf_op jit(solution)/shard_map/jit(take_along_axis)/gather | solution.py:64
  178.4 0.2 reshape.228
  178.5 0.1 copy.47
  178.7 0.0 all-gather.2.cloned.1.call-done
  178.7 5.1 %fusion = f32[1024]{0:T(1024)S(1)} fusion(bf16[1024,4096]{1,0:T(8,128)(2,1)} %all-gather.2.cloned.1.call-done), kind=kLoop, calls=%fused_computation.7 | loop fusion | flops 12581888 | bytes 8392704 | tf_op jit(solution)/shard_map/reduce_sum | solution.py:15
  183.8 10.2 %fusion.1 = bf16[1024,4096]{1,0:T(8,128)(2,1)} fusion(bf16[1024,4096]{1,0:T(8,128)(2,1)} %all-gather.2.cloned.1.call-done, f32[1024]{0:T(1024)S(1)} %add_sqrt_fusion.1), kind=kLoop, calls=%fused_computation.8 | loop fusion | flops 12582912 | bytes 16781312 | tf_op jit(solution)/shard_map/convert_element_type | solution.py:66
  194.0 8.4 %exponential_reduce_fusion = (f32[512]{0:T(512)S(1)}, f32[512,1024]{1,0:T(8,128)S(1)}) fusion(bf16[1024,4096]{1,0:T(8,128)(2,1)} %fusion.1, f32[512]{0:T(512)S(1)} %add_sqrt_fusion.2, bf16[512,4096]{1,0:T(8,128)(2,1)} %param.4), kind=kOutput, calls=%fused_computation.24 | convolution fusion | flops 4302306816 | bytes 14684160 | tf_op jit(solution)/shard_map/dot_general | solution.py:20
  202.4 4.5 %gather_fusion.2 = f32[512]{0:T(512)S(1)} fusion(f32[512,1024]{1,0:T(8,128)S(1)} %get-tuple-element.10, s32[512]{0:T(512)S(1)} %bitcast.19), kind=kCustom, calls=%fused_computation.2 | custom fusion | bytes 8192 | tf_op jit(solution)/shard_map/jit(take_along_axis)/gather | solution.py:70
  206.9 0.6 multiply_subtract_fusion
  207.5 9.6 %multiply_convert_fusion = bf16[1024,4096]{1,0:T(8,128)(2,1)} fusion(f32[512,1024]{1,0:T(8,128)S(1)} %get-tuple-element.10, f32[512]{0:T(512)S(1)} %get-tuple-element.6, s32[512]{0:T(512)S(1)} %copy-done.10, f32[512]{0:T(512)S(1)} %get-tuple-element.8, f32[512]{0:T(512)S(1)} %add_sqrt_fusion.2, bf16[512,4096]{1,0:T(8,128)(2,1)} %param.4), kind=kOutput, calls=%fused_computation.9 | convolution fusion | flops 4312268800 | bytes 14688256 | tf_op jit(solution)/shard_map/dot_general | solution.py:26
  217.2 0.0 reduce-scatter.2.cloned.1.call-update
  217.2 0.1 copy.48
  217.3 0.2 fusion.3
  217.5 0.5 copy-done.6
  218.0 0.1 eq.77
  218.1 0.1 copy.49
  218.2 3.6 %select_reduce_fusion = bf16[512,512]{1,0:T(8,128)(2,1)S(1)} fusion(f32[512,8]{1,0:T(8,128)S(1)} %copy.49, s32[512,8]{1,0:T(8,128)S(1)} %copy.48), kind=kLoop, calls=%fused_computation.17 | loop fusion | flops 6029312 | bytes 557056 | tf_op jit(solution)/shard_map/reduce_sum | solution.py:81
  221.9 0.8 copy-done.7
  222.7 7.0 %multiply_convert_fusion.1 = bf16[512,4096]{1,0:T(8,128)(2,1)} fusion(bf16[512,512]{1,0:T(8,128)(2,1)S(1)} %select_reduce_fusion, f32[512]{0:T(512)S(1)} %add_sqrt_fusion.2, bf16[512,4096]{1,0:T(8,128)(2,1)} %param.4), kind=kOutput, calls=%fused_computation.13 | convolution fusion | flops 2157969408 | bytes 8914944 | tf_op jit(solution)/shard_map/dot_general | solution.py:26
  229.7 7.5 %reshape.198 = bf16[128,4,4096]{2,1,0:T(4,128)(2,1)} reshape(bf16[512,4096]{1,0:T(8,128)(2,1)} %multiply_convert_fusion.1) | data formatting | bytes 8388608 | tf_op jit(solution)/shard_map/reshape | solution.py:101
  237.2 6.4 %all-to-all-start.2 = ((bf16[128,4,4096]{2,1,0:T(4,128)(2,1)}), bf16[128,4,4096]{2,1,0:T(4,128)(2,1)}, u32[]{:S(2)}, u32[]{:S(2)}) async-start(bf16[128,4,4096]{2,1,0:T(4,128)(2,1)} %reshape.198), calls=%async_computation.3 | async-start | bytes 8388608 | tf_op jit(solution)/shard_map/all_to_all | solution.py:103
  243.6 0.0 copy-start.2
  243.6 10.6 %fusion.19 = f32[512,4096]{1,0:T(8,128)} fusion(bf16[1024,4096]{1,0:T(8,128)(2,1)} %fusion.1, f32[512,1024]{1,0:T(8,128)S(1)} %get-tuple-element.10, f32[512]{0:T(512)S(1)} %get-tuple-element.6, s32[512]{0:T(512)S(1)} %copy-done.10, f32[512]{0:T(512)S(1)} %get-tuple-element.8), kind=kOutput, calls=%fused_computation.77 | convolution fusion | flops 4297588736 | bytes 18880512 | tf_op jit(solution)/shard_map/dot_general | solution.py:85
  254.2 5.7 %multiply_reduce_fusion = (f32[512]{0:T(512)S(1)}, f32[512,4096]{1,0:T(8,128)S(1)}) fusion(f32[512]{0:T(512)S(1)} %add_sqrt_fusion.2, bf16[512,4096]{1,0:T(8,128)(2,1)S(1)} %copy-done.2, f32[512,4096]{1,0:T(8,128)} %fusion.19, bf16[512,512]{1,0:T(8,128)(2,1)S(1)} %copy-done.8, bf16[512,4096]{1,0:T(8,128)(2,1)S(1)} %copy-done.4), kind=kOutput, calls=%fused_computation.15 | convolution fusion | flops 2160066048 | bytes 25694208 | tf_op jit(solution)/shard_map/dot_general | solution.py:86
  259.9 4.0 %divide_convert_fusion = bf16[512,4096]{1,0:T(8,128)(2,1)} fusion(f32[512,4096]{1,0:T(8,128)S(1)} %get-tuple-element.12, f32[512]{0:T(512)S(1)} %get-tuple-element.11, f32[512]{0:T(512)S(1)} %add_sqrt_fusion.2, bf16[512,4096]{1,0:T(8,128)(2,1)S(1)} %copy-done.2), kind=kLoop, calls=%fused_computation.14 | loop fusion | flops 12582912 | bytes 16781312 | tf_op jit(solution)/shard_map/convert_element_type | solution.py:91
  264.0 41.9 %all-to-all-done.2 = bf16[128,4,4096]{2,1,0:T(4,128)(2,1)} async-done(((bf16[128,4,4096]{2,1,0:T(4,128)(2,1)}), bf16[128,4,4096]{2,1,0:T(4,128)(2,1)}, u32[]{:S(2)}, u32[]{:S(2)}) %all-to-all-start.2) | async-done | bytes 4194336 | tf_op jit(solution)/shard_map/all_to_all | solution.py:103
  305.9 6.9 %reshape.199 = bf16[512,4096]{1,0:T(8,128)(2,1)} reshape(bf16[128,4,4096]{2,1,0:T(4,128)(2,1)} %all-to-all-done.2) | data formatting | bytes 8388608 | tf_op jit(solution)/shard_map/reshape | solution.py:105
  312.8 35.7 %reduce-scatter.2.cloned.1.call-done = bf16[64,4096]{1,0:T(8,128)(2,1)} async-done(((bf16[1024,4096]{1,0:T(8,128)(2,1)}), bf16[64,4096]{1,0:T(8,128)(2,1)}) %reduce-scatter.2.cloned.1.call-update) | async-done | bytes 524304 | tf_op jit(solution)/shard_map/reduce_scatter | solution.py:92
  348.5 3.3 multiply_reduce_fusion.2
  351.8 1.1 divide_convert_fusion.2
  (37 shorter events, 0.3 us)
Async XLA Ops:
  7.2 47.0 %copy-start = (bf16[64,4096]{1,0:T(8,128)(2,1)S(1)}, bf16[64,4096]{1,0:T(8,128)(2,1)}, u32[]{:S(2)}) copy-start(bf16[64,4096]{1,0:T(8,128)(2,1)} %param.5) | copy-start | bytes 1572868
  7.2 171.5 %all-gather.2.cloned.1.call-start = ((), (), s32[]{:S(2)}) async-start(), calls=%async_computation.4 | async-start | bytes 8912896 | tf_op jit(solution)/shard_map/all_gather | solution.py:65
  52.7 5.9 %copy-start.5 = (s32[128,1,4]{2,1,0:T(1,128)}, s32[128,1,4]{2,1,0:T(1,128)S(1)}, u32[]{:S(2)}) copy-start(s32[128,1,4]{2,1,0:T(1,128)S(1)} %all_to_all.19) | copy-start | bytes 6148
  65.8 58.3 %all-to-all-start.1 = ((bf16[128,4,4096]{2,1,0:T(4,128)(2,1)}), bf16[128,4,4096]{2,1,0:T(4,128)(2,1)}, u32[]{:S(2)}, u32[]{:S(2)}) async-start(bf16[128,4,4096]{2,1,0:T(4,128)(2,1)} %reshape.196), calls=%async_computation.1 | async-start | bytes 8388608 | tf_op jit(solution)/shard_map/all_to_all | solution.py:59
  71.4 277.0 %reduce-scatter.2.cloned.1.call-start = ((), (), s32[]{:S(2)}) async-start(), calls=%async_computation.5 | async-start | bytes 8912896 | tf_op jit(solution)/shard_map/reduce_scatter | solution.py:92
  71.9 23.3 %copy-start.9 = (s32[512,8]{0,1:T(8,128)S(1)}, s32[512,8]{0,1:T(8,128)}, u32[]{:S(2)}) copy-start(s32[512,8]{0,1:T(8,128)} %param.7) | copy-start | bytes 49156
  71.9 23.6 %copy-start.10 = (s32[512]{0:T(512)S(1)}, s32[512]{0:T(512)}, u32[]{:S(2)}) copy-start(s32[512]{0:T(512)} %param.6) | copy-start | bytes 6148
  136.2 6.8 %copy-start.1 = (bf16[512,4096]{1,0:T(8,128)(2,1)S(1)}, bf16[512,4096]{1,0:T(8,128)(2,1)}, u32[]{:S(2)}) copy-start(bf16[512,4096]{1,0:T(8,128)(2,1)} %param.4) | copy-start | bytes 12582916
  141.0 2.0 copy-start.3
  217.2 0.8 copy-start.6
  221.9 0.8 copy-start.7
  237.2 68.7 %all-to-all-start.2 = ((bf16[128,4,4096]{2,1,0:T(4,128)(2,1)}), bf16[128,4,4096]{2,1,0:T(4,128)(2,1)}, u32[]{:S(2)}, u32[]{:S(2)}) async-start(bf16[128,4,4096]{2,1,0:T(4,128)(2,1)} %reshape.198), calls=%async_computation.3 | async-start | bytes 8388608 | tf_op jit(solution)/shard_map/all_to_all | solution.py:103
  243.6 10.6 %copy-start.2 = (bf16[512,4096]{1,0:T(8,128)(2,1)S(1)}, bf16[512,4096]{1,0:T(8,128)(2,1)}, u32[]{:S(2)}) copy-start(bf16[512,4096]{1,0:T(8,128)(2,1)} %param.4) | copy-start | bytes 12582916
  243.6 10.6 %copy-start.4 = (bf16[512,4096]{1,0:T(8,128)(2,1)S(1)}, bf16[512,4096]{1,0:T(8,128)(2,1)}, u32[]{:S(2)}) copy-start(bf16[512,4096]{1,0:T(8,128)(2,1)} %copy-done.3) | copy-start | bytes 12582916
  243.6 10.6 %copy-start.8 = (bf16[512,512]{1,0:T(8,128)(2,1)S(1)}, bf16[512,512]{1,0:T(8,128)(2,1)}, u32[]{:S(2)}) copy-start(bf16[512,512]{1,0:T(8,128)(2,1)} %copy-done.7) | copy-start | bytes 1572868
Sparse Core Ops, SparseCore 0:
  10.5 117.7 all-gather.1
  217.3 131.1 reduce-scatter.1
where the time goes:
time: 361 us; the launch traced here: 360 us
  waiting for transfers between devices  104 us (29%)
  local copies, waits for them, and re-layouts  101 us (28%)
  other arithmetic  60.8 us (17%)
  matrix products  47 us (13%)
  blocking collectives  20.8 us (6%)
  between operations  14.4 us (4%)
  starting transfers between devices  12.3 us (3%)
    all_to_all x1, waiting for transfers between devices, shards(): lax.all_to_all(slot_sums, ('blk', 'group'), split_axis=0, concat_axis=0,...  41.9 us
    reduce_scatter x1, waiting for transfers between devices, shards(): lax.psum_scatter((logit_scale * contract_cols(cycle_weight, query_hat)).a...  35.7 us
    gather x5, local copies, waits for them, and re-layouts, shards(): hard_scores = jnp.take_along_axis(slot_scores, slot_index, axis=1)  33.5 us
    all_to_all x1, waiting for transfers between devices, shards(): lax.all_to_all(outgoing, ('blk', 'group'), split_axis=0, concat_axis=0, t...  25.4 us
    gather x1, local copies, waits for them, and re-layouts, shards(): ranked.reshape(-1)[flat_ids].reshape(owners.shape)  23 us
    another operation x1, other arithmetic, shards(): wanted = jnp.zeros((peers * passage_count,), jnp.int32).at[flat_ids].max(...  22.4 us
    all_to_all x1, blocking collectives, shards(): lax.all_to_all(local_table, ('blk', 'group'), split_axis=0, concat_axis=0...  20.8 us
    dot_general x2, matrix products, contract_cols(): lax.dot_general(left, right, (((0,), (0,)), ((), ())), preferred_element_...  16.6 us
  transfers between devices with their start and end apart: 4, of which 3 were waited for; matrix products, arithmetic and copies ran while one was open for 45% of the time, Pallas kernels for 0%

commit v1 on v0

v1 whole, which is shorter than its diff:
```python
import jax
import jax.numpy as jnp
from jax import lax
from jax.experimental import pallas as pl
from jax.experimental.pallas import tpu as pltpu
from jax.sharding import PartitionSpec as P

D = 4096
Q = 512
PB = 64
HARD = 8
CAP = 4
SCALE = 20.0
EPS = 1e-06
CH = 256
SL = 128
PARTS = 2
PW = D // PARTS
TN = 512
FWD_STEPS = ((0, 0), (0, 1), (1, 0), (3, 0), (1, 1), (3, 1), (2, 0), (2, 1))
BWD_STEPS = ((2, 0), (2, 1), (1, 0), (3, 0), (1, 1), (3, 1), (0, 0), (0, 1))
MESH = pl.DeviceIdType.MESH
F32 = jnp.float32
BF16 = jnp.bfloat16
NT = (((1,), (1,)), ((), ()))
TN_DIMS = (((0,), (0,)), ((), ()))


def iota(shape, dim):
    return lax.broadcasted_iota(jnp.int32, shape, dim)


def inv_rel(rel):
    return ((4 - rel // 2) % 4) * 2 + rel % 2


def dot(a, b):
    return jnp.dot(a, b, preferred_element_type=F32)


def onehot(mask):
    return jnp.where(mask, 1.0, 0.0).astype(BF16)


def kernel(
    passages, queries, ids_ref, out_q, out_p, out_l,
    pv, qv, qhat, hat, fsend, fetched, sret, part, sibr, z2m, z2p, z1m, z1p, xr,
    exp_c, exp_h, wc, wct, wh, wht, qsum, sel, selt, tabs, qinv, key_ref, kk_ref,
    lsem, ag_s, ag_r, tab_s, tab_r, f_s, f_r, r_s, r_r, rs_s, rs_r,
):
    blk = lax.axis_index("blk")
    grp = lax.axis_index("group")
    xh, z, core = blk // 8, (blk // 2) % 4, blk % 2
    y, xl = grp // 2, grp % 2

    def dev(dxh=0, dz=0, dc=0, dy=0, dxl=0):
        return (
            ((xh + dxh) % 2) * 8 + ((z + dz) % 4) * 2 + (core + dc) % 2,
            ((y + dy) % 4) * 2 + (xl + dxl) % 2,
        )

    sib, zp, zm, xo = dev(dc=1), dev(dz=1), dev(dz=3), dev(dxh=1)
    partner = [
        dev(dy=rel // 2, dxl=rel % 2, dxh=(rel % 2) & (rel // 2 % 2)) for rel in range(8)
    ]

    barrier = pltpu.get_barrier_semaphore()
    for d in [sib, zp, zm, xo] + partner[1:]:
        pl.semaphore_signal(barrier, inc=1, device_id=d, device_id_type=MESH)

    load_p = pltpu.make_async_copy(passages, pv, lsem.at[0])
    load_q = pltpu.make_async_copy(queries, qv, lsem.at[1])
    load_p.start()
    load_q.start()

    def remote(src, dst, ss, rs, d):
        return pltpu.make_async_remote_copy(
            src_ref=src, dst_ref=dst, send_sem=ss, recv_sem=rs, device_id=d, device_id_type=MESH
        )

    def cols(part_id):
        return pl.ds(part_id * PW, PW)

    ag = {}

    def row(dz, dc, dxh):
        return dz * CH + dc * 2 * PB + dxh * PB

    def add_ag(name, src, dst, d, parts=(0, 1)):
        for cq in parts:
            i = len(ag)
            ag[name, cq] = remote(
                hat.at[pl.ds(src, PB), cols(cq)], hat.at[pl.ds(dst, PB), cols(cq)],
                ag_s.at[i], ag_r.at[i], d,
            )

    own = row(0, 0, 0)
    add_ag("x", own, row(0, 0, 1), xo)
    add_ag("m0", own, row(3, 0, 0), zp)
    add_ag("p0", own, row(1, 0, 0), zm)
    add_ag("s00", own, row(0, 1, 0), sib)
    add_ag("s01", row(0, 0, 1), row(0, 1, 1), sib)
    add_ag("m1", row(0, 0, 1), row(3, 0, 1), zp)
    add_ag("p1", row(0, 0, 1), row(1, 0, 1), zm)
    for dxh in range(2):
        add_ag(f"s3{dxh}", row(3, 0, dxh), row(3, 1, dxh), sib)
        add_ag(f"s1{dxh}", row(1, 0, dxh), row(1, 1, dxh), sib)
        add_ag(f"t{dxh}", row(3, 0, dxh), row(2, 0, dxh), zp, (0,))
        add_ag(f"t{dxh}", row(1, 0, dxh), row(2, 0, dxh), zm, (1,))
        add_ag(f"s2{dxh}", row(2, 0, dxh), row(2, 1, dxh), sib)

    fetch, back = {}, {}
    for step, (j, cq) in enumerate(FWD_STEPS):
        for rel in range(1, 8):
            to = inv_rel(rel)
            fetch[j, cq, rel] = remote(
                fsend.at[pl.ds(j * SL + rel * 16, 16), cols(cq)],
                fetched.at[pl.ds(j * SL + to * 16, 16), cols(cq)],
                f_s.at[step, rel], f_r.at[step, to], partner[rel],
            )
    for step, (j, cq) in enumerate(BWD_STEPS):
        for rel in range(1, 8):
            to = inv_rel(rel)
            back[j, cq, rel] = remote(
                fsend.at[pl.ds(j * SL + rel * 16, 16), cols(cq)],
                sret.at[pl.ds(j * SL + to * 16, 16), cols(cq)],
                r_s.at[step, rel], r_r.at[step, to], partner[rel],
            )

    rs = {}

    def add_rs(name, src, dst, d):
        i = len(rs)
        rs[name] = remote(src, dst, rs_s.at[i], rs_r.at[i], d)

    for j, cq in BWD_STEPS:
        add_rs(
            ("sib", j, cq),
            part.at[pl.ds(j * CH + SL, SL), cols(cq)], sibr.at[pl.ds(j * SL, SL), cols(cq)], sib,
        )
    add_rs(("z", 2, 0), part.at[pl.ds(2 * CH, SL), cols(0)], z2m, zp)
    add_rs(("z", 2, 1), part.at[pl.ds(2 * CH, SL), cols(1)], z2p, zm)
    for cq in range(PARTS):
        add_rs(("z", 1, cq), part.at[pl.ds(CH, SL), cols(cq)], z1m.at[:, cols(cq)], zp)
        add_rs(("z", 3, cq), part.at[pl.ds(3 * CH, SL), cols(cq)], z1p.at[:, cols(cq)], zm)
        add_rs(("x", cq), part.at[pl.ds(PB, PB), cols(cq)], xr.at[:, cols(cq)], xo)

    load_p.wait()
    raw = pv[...].astype(F32)
    pinv = 1.0 / jnp.sqrt(jnp.sum(raw * raw, axis=1, keepdims=True) + EPS)
    hat[pl.ds(own, PB), :] = (raw * pinv).astype(BF16)
    pl.semaphore_wait(barrier, 11)
    for cq in range(PARTS):
        for name in ("x", "m0", "p0", "s00"):
            ag[name, cq].start()

    ids = ids_ref[...]
    owner = lax.shift_right_logical(ids, 6)
    ob, og = lax.shift_right_logical(owner, 3), owner & 7
    rel_g = ((lax.shift_right_logical(og, 1) - y) & 3) * 2 + ((og & 1) ^ xl)
    rel_b = (
        ((lax.shift_right_logical(ob, 1) - z) & 3) * 4
        + ((ob & 1) ^ core) * 2
        + (lax.shift_right_logical(ob, 3) ^ xh)
    )
    keys = (rel_g * 16 + rel_b) * 64 + (ids & 63)
    key_ref[...] = keys
    count = jnp.zeros((128, 128), F32)
    lane_q = iota((Q, 128), 1)
    for h in range(HARD):
        column = keys[:, h : h + 1]
        hi = onehot(lax.shift_right_logical(column, 6) == lane_q)
        lo = onehot((column & 63) == lane_q)
        count = count + lax.dot_general(lo, hi, TN_DIMS, preferred_element_type=F32)
    present = count > 0.5
    sub = iota((128, 128), 0)
    rank = dot(onehot(iota((128, 128), 1) < sub), onehot(present))
    table = jnp.zeros((8, 128), F32)
    for slot in range(CAP):
        hit = jnp.where(
            jnp.logical_and(present, rank == float(slot)), (sub + 1).astype(F32), 0.0
        )
        found = jnp.sum(hit, axis=0, keepdims=True) - 1.0
        table = jnp.where(iota((8, 128), 0) == slot, found, table)
    tabs[0] = table
    ask = []
    for rel in range(1, 8):
        to = inv_rel(rel)
        ask.append(remote(tabs.at[0], tabs.at[to], tab_s.at[rel], tab_r.at[to], partner[rel]))
        ask[-1].start()

    load_q.wait()

    def norm_rows(i, carry):
        rows = pl.ds(pl.multiple_of(i * 32, 32), 32)
        values = qv[rows, :].astype(F32)
        inverse = 1.0 / jnp.sqrt(jnp.sum(values * values, axis=1, keepdims=True) + EPS)
        qinv[rows, :] = jnp.broadcast_to(inverse, (32, 128))
        qhat[rows, :] = (values * inverse).astype(BF16)
        return carry

    def norm_queries(first, last):
        lax.fori_loop(first, last, norm_rows, 0)

    def build_selection():
        everything = tabs[...].reshape(64, 128).astype(BF16)
        lane = iota((128, 128), 1)
        who, o, slot = lane >> 4, (lane >> 2) & 3, lane & 3
        back_rel = ((4 - (who >> 1)) & 3) * 2 + (who & 1)
        flip = (who & 1) & ((who >> 1) & 1)
        offset = (o >> 1) * 128 + ((o & 1) ^ flip) * 64
        diag = iota((64, 128), 0) == (who * 8 + slot)[:64]
        for j in range(4):
            pick = onehot(iota((128, 128), 0) == back_rel * 16 + j * 4 + o)
            local = jnp.sum(jnp.where(diag, dot(everything, pick), 0.0), axis=0, keepdims=True)
            target = jnp.where(local >= 0.0, local + offset[:1].astype(F32), -1.0)
            match = jnp.where(iota((CH, SL), 0).astype(F32) == target, 1.0, 0.0)
            selt[pl.ds(j * CH, CH), :] = match.astype(BF16)
            sel[pl.ds(j * SL, SL), :] = jnp.transpose(match).astype(BF16)

    def build_mask():
        lane = iota((128, Q), 1)
        from_lane = ((lane >> 4) & 7) * 16 + (lane >> 7) * 4 + ((lane >> 2) & 3)
        spread = dot(table.astype(BF16), onehot(iota((128, Q), 0) == from_lane))
        local = jnp.sum(
            jnp.where(iota((8, Q), 0) == (lane & 3)[:8], spread, 0.0), axis=0, keepdims=True
        )
        wanted = jnp.where(local >= 0.0, from_lane[:1] * 64 + local.astype(jnp.int32), -1)

        def rows_mask(i, carry):
            rows = pl.ds(pl.multiple_of(i * 64, 64), 64)
            mine = key_ref[rows, :]
            found = mine[:, 0:1] == wanted
            for h in range(1, HARD):
                found = jnp.logical_or(found, mine[:, h : h + 1] == wanted)
            exp_h[rows, :] = jnp.where(found, 1.0, 0.0)
            return carry

        lax.fori_loop(0, Q // 64, rows_mask, 0)

    def select(j, cq):
        def tile(n, carry):
            at = pl.ds(pl.multiple_of(cq * PW + n * TN, TN), TN)
            rows = dot(sel[pl.ds(j * SL, SL), :], hat[pl.ds(j * CH, CH), at]).astype(BF16)
            fsend[pl.ds(j * SL, SL), at] = rows
            fetched[pl.ds(j * SL, 16), at] = rows[:16]
            return carry

        lax.fori_loop(0, PW // TN, tile, 0)
        for rel in range(1, 8):
            fetch[j, cq, rel].start()

    totals = {"cycle": jnp.zeros((Q, 1), F32), "pos": jnp.zeros((Q, 1), F32)}

    def cycle_scores(j):
        scores = SCALE * lax.dot_general(
            qhat[...], hat[pl.ds(j * CH, CH), :], NT, preferred_element_type=F32
        )
        raised = jnp.exp(scores)
        exp_c[:, pl.ds(j * CH, CH)] = raised
        positive = kk_ref[...] == iota((Q, CH), 1) + j * CH
        totals["cycle"] = totals["cycle"] + jnp.sum(raised, axis=1, keepdims=True)
        totals["pos"] = totals["pos"] + jnp.sum(
            jnp.where(positive, scores, 0.0), axis=1, keepdims=True
        )

    positives = ids[:, HARD : HARD + 1]
    pb = lax.shift_right_logical(positives, 6)
    kk_ref[...] = (
        ((lax.shift_right_logical(pb, 1) - z) & 3) * CH
        + ((pb & 1) ^ core) * 128
        + (lax.shift_right_logical(pb, 3) ^ xh) * 64
        + (positives & 63)
    )

    def relay_x(cq):
        ag["x", cq].wait_recv()
        for name in ("s01", "m1", "p1"):
            ag[name, cq].start()

    def relay_z(dxh, cq):
        ag[f"m{dxh}", cq].wait_recv()
        ag[f"s3{dxh}", cq].start()
        if cq == 0:
            ag[f"t{dxh}", 0].start()
        ag[f"p{dxh}", cq].wait_recv()
        ag[f"s1{dxh}", cq].start()
        if cq == 1:
            ag[f"t{dxh}", 1].start()

    def relay_two(dxh, cq):
        ag[f"t{dxh}", cq].wait_recv()
        ag[f"s2{dxh}", cq].start()

    def from_sib(j, cq):
        for dxh in range(2):
            ag[f"s{j}{dxh}", cq].wait_recv()

    for copy in ask:
        copy.wait_recv()
    build_selection()
    norm_queries(0, 6)
    relay_x(0)
    relay_z(0, 0)
    from_sib(0, 0)
    select(0, 0)
    norm_queries(6, 16)
    relay_x(1)
    relay_z(0, 1)
    from_sib(0, 1)
    select(0, 1)
    cycle_scores(0)
    relay_z(1, 0)
    from_sib(1, 0)
    select(1, 0)
    from_sib(3, 0)
    select(3, 0)
    relay_two(0, 0)
    relay_two(0, 1)
    relay_z(1, 1)
    from_sib(1, 1)
    select(1, 1)
    from_sib(3, 1)
    select(3, 1)
    cycle_scores(1)
    relay_two(1, 0)
    relay_two(1, 1)
    from_sib(2, 0)
    select(2, 0)
    from_sib(2, 1)
    select(2, 1)
    cycle_scores(3)
    cycle_scores(2)
    build_mask()

    pos_score = totals["pos"]
    pos_exp = jnp.exp(pos_score)
    hard_total = pos_exp
    for j in (0, 1, 3, 2):
        for cq in range(PARTS):
            for rel in range(1, 8):
                fetch[j, cq, rel].wait_recv()
        at = pl.ds(j * SL, SL)
        scores = SCALE * lax.dot_general(
            qhat[...], fetched[at, :], NT, preferred_element_type=F32
        )
        raised = exp_h[:, at] * jnp.exp(scores)
        exp_h[:, at] = raised
        hard_total = hard_total + jnp.sum(raised, axis=1, keepdims=True)
    for copy in fetch.values():
        copy.wait_send()
    hard_inv = 1.0 / hard_total

    def back_step(j, cq):
        def tile(n, carry):
            at = pl.ds(pl.multiple_of(cq * PW + n * TN, TN), TN)
            rows = (SCALE * dot(wht[pl.ds(j * SL, SL), :], qhat[:, at])).astype(BF16)
            fsend[pl.ds(j * SL, SL), at] = rows
            sret[pl.ds(j * SL, 16), at] = rows[:16]
            return carry

        lax.fori_loop(0, PW // TN, tile, 0)
        for rel in range(1, 8):
            back[j, cq, rel].start()

    for j in (2, 1, 3, 0):
        weights = exp_h[:, pl.ds(j * SL, SL)] * hard_inv
        wh[:, pl.ds(j * SL, SL)] = weights.astype(BF16)
        wht[pl.ds(j * SL, SL), :] = jnp.transpose(weights).astype(BF16)
    for j, cq in BWD_STEPS:
        back_step(j, cq)

    cycle_total = totals["cycle"]
    out_l[...] = jnp.log(cycle_total) + jnp.log(hard_total) - 2.0 * pos_score
    cycle_inv = 1.0 / cycle_total
    correction = 2.0 - pos_exp * hard_inv
    for j in (2, 1, 3, 0):
        at = pl.ds(j * CH, CH)
        positive = kk_ref[...] == iota((Q, CH), 1) + j * CH
        weights = exp_c[:, at] * cycle_inv - jnp.where(positive, correction, 0.0)
        wc[:, at] = weights.astype(BF16)
        wct[at, :] = jnp.transpose(weights).astype(BF16)

    QR = 128
    store_q = []

    def query_rows(block):
        rows = pl.ds(block * QR, QR)
        inverse = qinv[rows, 0:1]

        def product(n, total):
            at = pl.ds(pl.multiple_of(n * TN, TN), TN)
            tile = SCALE * (dot(wc[rows, :], hat[:, at]) + dot(wh[rows, :], fetched[:, at]))
            qsum[:, at] = tile
            unit = qv[rows, at].astype(F32) * inverse
            return total + jnp.sum(unit * tile, axis=1, keepdims=True)

        along = lax.fori_loop(0, D // TN, product, jnp.zeros((QR, 1), F32))

        def project(n, carry):
            at = pl.ds(pl.multiple_of(n * TN, TN), TN)
            unit = qv[rows, at].astype(F32) * inverse
            qv[rows, at] = ((qsum[:, at] - unit * along) * inverse).astype(BF16)
            return carry

        lax.fori_loop(0, D // TN, project, 0)
        store_q.append(
            pltpu.make_async_copy(qv.at[rows, :], out_q.at[rows, :], lsem.at[2 + block])
        )
        store_q[-1].start()

    def partial(j, cq):
        for rel in range(1, 8):
            back[j, cq, rel].wait_recv()

        def tile(n, carry):
            at = pl.ds(pl.multiple_of(cq * PW + n * TN, TN), TN)
            total = SCALE * dot(wct[pl.ds(j * CH, CH), :], qhat[:, at]) + dot(
                selt[pl.ds(j * CH, CH), :], sret[pl.ds(j * SL, SL), at]
            )
            part[pl.ds(j * CH, CH), at] = total.astype(BF16)
            return carry

        lax.fori_loop(0, PW // TN, tile, 0)
        rs["sib", j, cq].start()

    def reduce(j, cq):
        at = cols(cq)
        mine = pl.ds(j * CH, SL)
        rs["sib", j, cq].wait_recv()
        total = part[mine, at].astype(F32) + sibr[pl.ds(j * SL, SL), at].astype(F32)
        if (j, cq) == (1, 0):
            rs["z", 2, 0].wait_recv()
            total = total + z2m[...].astype(F32)
        if (j, cq) == (3, 1):
            rs["z", 2, 1].wait_recv()
            total = total + z2p[...].astype(F32)
        if j == 0:
            rs["z", 1, cq].wait_recv()
            rs["z", 3, cq].wait_recv()
            total = total + z1m[:, at].astype(F32) + z1p[:, at].astype(F32)
        part[mine, at] = total.astype(BF16)
        if j == 0:
            rs["x", cq].start()
        else:
            rs["z", j, cq].start()

    query_rows(0)
    partial(2, 0)
    partial(2, 1)
    reduce(2, 0)
    reduce(2, 1)
    query_rows(1)
    partial(1, 0)
    partial(3, 0)
    reduce(1, 0)
    reduce(3, 0)
    query_rows(2)
    partial(1, 1)
    partial(3, 1)
    reduce(1, 1)
    reduce(3, 1)
    query_rows(3)
    partial(0, 0)
    partial(0, 1)
    reduce(0, 0)
    reduce(0, 1)

    unit = pv[...].astype(F32) * pinv
    for cq in range(PARTS):
        rs["x", cq].wait_recv()
    total = part[pl.ds(0, PB), :].astype(F32) + xr[...].astype(F32)
    along = jnp.sum(unit * total, axis=1, keepdims=True)
    out_p[...] = ((total - unit * along) * pinv).astype(BF16)

    for copy in ask + list(ag.values()) + list(back.values()) + list(rs.values()):
        copy.wait_send()
    for copy in store_q:
        copy.wait()


def shards(queries, passages, positives, hard_ids):
    ids = jnp.concatenate([hard_ids, positives[:, None]], axis=1)
    dma = pltpu.SemaphoreType.DMA
    any_spec = pl.BlockSpec(memory_space=pl.ANY)
    vmem_spec = pl.BlockSpec(memory_space=pltpu.VMEM)
    query_grads, passage_grads, losses = pl.pallas_call(
        kernel,
        out_shape=(
            jax.ShapeDtypeStruct((Q, D), BF16),
            jax.ShapeDtypeStruct((PB, D), BF16),
            jax.ShapeDtypeStruct((Q, 1), F32),
        ),
        in_specs=[any_spec, any_spec, vmem_spec],
        out_specs=(any_spec, vmem_spec, vmem_spec),
        scratch_shapes=[
            pltpu.VMEM((PB, D), BF16),
            pltpu.VMEM((Q, D), BF16),
            pltpu.VMEM((Q, D), BF16),
            pltpu.VMEM((4 * CH, D), BF16),
            pltpu.VMEM((4 * SL, D), BF16),
            pltpu.VMEM((4 * SL, D), BF16),
            pltpu.VMEM((4 * SL, D), BF16),
            pltpu.VMEM((4 * CH, D), BF16),
            pltpu.VMEM((4 * SL, D), BF16),
            pltpu.VMEM((SL, PW), BF16),
            pltpu.VMEM((SL, PW), BF16),
            pltpu.VMEM((SL, D), BF16),
            pltpu.VMEM((SL, D), BF16),
            pltpu.VMEM((PB, D), BF16),
            pltpu.VMEM((Q, 4 * CH), F32),
            pltpu.VMEM((Q, 4 * SL), F32),
            pltpu.VMEM((Q, 4 * CH), BF16),
            pltpu.VMEM((4 * CH, Q), BF16),
            pltpu.VMEM((Q, 4 * SL), BF16),
            pltpu.VMEM((4 * SL, Q), BF16),
            pltpu.VMEM((128, D), F32),
            pltpu.VMEM((4 * SL, CH), BF16),
            pltpu.VMEM((4 * CH, SL), BF16),
            pltpu.VMEM((8, 8, 128), F32),
            pltpu.VMEM((Q, 128), F32),
            pltpu.VMEM((Q, HARD + 1), jnp.int32),
            pltpu.VMEM((Q, 1), jnp.int32),
            dma((8,)),
            dma((32,)), dma((32,)),
            dma((8,)), dma((8,)),
            dma((8, 8)), dma((8, 8)),
            dma((8, 8)), dma((8, 8)),
            dma((16,)), dma((16,)),
        ],
        compiler_params=pltpu.CompilerParams(
            collective_id=0, has_side_effects=True, vmem_limit_bytes=63 * 2**20
        ),
        cost_estimate=pl.CostEstimate(
            flops=6 * Q * 1536 * D, bytes_accessed=4 * Q * D, transcendentals=Q * 1536
        ),
    )(passages, queries, ids)
    return query_grads, passage_grads, losses.reshape(Q)


def solution(mesh):
    in_specs = (
        P(("blk", "group"), None),
        P(("blk", "group"), None),
        P(("blk", "group")),
        P(("blk", "group"), None),
    )
    out_specs = (P(("blk", "group"), None), P(("blk", "group"), None), P(("blk", "group")))
    return jax.shard_map(shards, mesh=mesh, in_specs=in_specs, out_specs=out_specs, check_vma=False)
```

time: 361 us -> 170 us (0.47)
  Pallas kernels: 0 us -> 160 us
  waiting for transfers between devices: 104 us -> 0 us
  local copies, waits for them, and re-layouts: 101 us -> 6.41 us
  other arithmetic: 60.8 us -> 2.42 us
  matrix products: 47 us -> 0 us
  blocking collectives: 20.8 us -> 0 us
  between operations: 14.4 us -> 0.64 us
  starting transfers between devices: 12.3 us -> 0 us
    pallas_call x0 -> x1, Pallas kernels: none -> 160 us  [shards(): pl.pallas_call(kernel, out_shape=(jax.ShapeDtypeStruct((Q, D), BF16), jax...]
    all_to_all x2 -> x0, waiting for transfers between devices: 67.3 us -> none  [the longest x1 41.9 us: shards(): lax.all_to_all(slot_sums, ('blk', 'group'), split_axis=0, concat_axis=0,...]
    gather x8 -> x0, local copies, waits for them, and re-layouts: 65.4 us -> none  [the longest x5 33.5 us: shards(): hard_scores = jnp.take_along_axis(slot_scores, slot_index, axis=1)]
    dot_general x7 -> x0, matrix products: 47 us -> none  [the longest x2 16.6 us: contract_cols(): lax.dot_general(left, right, (((0,), (0,)), ((), ())), preferred_element_...]
    reduce_scatter x1 -> x0, waiting for transfers between devices: 35.7 us -> none  [shards(): lax.psum_scatter((logit_scale * contract_cols(cycle_weight, query_hat)).a...]
    another operation x2 -> x0, other arithmetic: 22.5 us -> none  [the longest x1 22.4 us: shards(): wanted = jnp.zeros((peers * passage_count,), jnp.int32).at[flat_ids].max(...]
    reshape x9 -> x0, local copies, waits for them, and re-layouts: 22.3 us -> none  [the longest x1 7.52 us: shards(): slot_sums = (logit_scale * contract_cols(weight_table, query_hat)).astype...]
    all_to_all x1 -> x0, blocking collectives: 20.8 us -> none  [shards(): lax.all_to_all(local_table, ('blk', 'group'), split_axis=0, concat_axis=0...]
  transfers between devices with their start and end apart: 4 -> 0, of which waited for: 3 -> 0; matrix products, arithmetic and copies ran while one was open for 45% -> 0% of each run, Pallas kernels for 0% -> 0%
where the time goes in v1:
time: 170 us
  Pallas kernels  160 us (94%)
  local copies, waits for them, and re-layouts  6.41 us (4%)
  other arithmetic  2.42 us (1%)
    pallas_call x1, Pallas kernels, shards(): pl.pallas_call(kernel, out_shape=(jax.ShapeDtypeStruct((Q, D), BF16), jax...  160 us
    unnamed x4, local copies, waits for them, and re-layouts  5.55 us

profile of v1, /device:TPU:1, one launch (start us, length us, event | category | flops | bytes accessed | tf_op | source)
XLA Modules:
  0.0 169.9 jit_solution(7054151145462625318)
XLA Ops:
  0.6 0.7 pad_add_fusion
  1.4 0.9 copy.10.ids_ref
  2.2 160.4 %shard_map.67 = (bf16[512,4096]{1,0:T(8,128)(2,1)}, bf16[64,4096]{1,0:T(8,128)(2,1)}, f32[512,1]{1,0:T(8,128)}) custom-call(bf16[64,4096]{1,0:T(8,128)(2,1)} %passages.1, bf16[512,4096]{1,0:T(8,128)(2,1)} %queries.1, s32[512,9]{1,0:T(8,128)} %copy.10.ids_ref), custom_call_target="tpu_custom_call" | custom-call | flops 19327352832 | bytes 8388608 | tf_op jit(solution)/shard_map/pallas_call | solution.py:487
  162.6 1.7 reduce
  164.3 0.0 copy-start
  164.3 4.8 %copy.13 = bf16[512,4096]{1,0:T(8,128)(2,1)} copy(bf16[512,4096]{1,0:T(8,128)(2,1)} %get-tuple-element.12) | data formatting | bytes 8388608
  169.1 0.0 copy-done
  169.1 0.8 copy.14
Async XLA Ops:
  164.3 4.8 %copy-start = (bf16[64,4096]{1,0:T(8,128)(2,1)S(1)}, bf16[64,4096]{1,0:T(8,128)(2,1)}, u32[]{:S(2)}) copy-start(bf16[64,4096]{1,0:T(8,128)(2,1)} %get-tuple-element.13) | copy-start | bytes 1572868

commit v2 on v1

--- a/solution.py
+++ b/solution.py
@@ -14,11 +14,14 @@
 EPS = 1e-06
 CH = 256
 SL = 128
-PARTS = 2
+PARTS = 4
 PW = D // PARTS
 TN = 512
-FWD_STEPS = ((0, 0), (0, 1), (1, 0), (3, 0), (1, 1), (3, 1), (2, 0), (2, 1))
-BWD_STEPS = ((2, 0), (2, 1), (1, 0), (3, 0), (1, 1), (3, 1), (0, 0), (0, 1))
+HALF = PARTS // 2
+ALL_PARTS = tuple(range(PARTS))
+DEPTH = 3
+STEPS = 4 * PARTS
+BWD_STEPS = tuple((j, cq) for j in (3, 2, 1, 0) for cq in ALL_PARTS)
 MESH = pl.DeviceIdType.MESH
 F32 = jnp.float32
 BF16 = jnp.bfloat16
@@ -34,6 +37,14 @@
     return ((4 - rel // 2) % 4) * 2 + rel % 2
 
 
+def flips(rel):
+    return (rel % 2) & (rel // 2 % 2)
+
+
+def seen_by(rel, j):
+    return (0, 2, 1, 3)[j] if flips(rel) else j
+
+
 def dot(a, b):
     return jnp.dot(a, b, preferred_element_type=F32)
 
@@ -44,7 +55,7 @@
 
 def kernel(
     passages, queries, ids_ref, out_q, out_p, out_l,
-    pv, qv, qhat, hat, fsend, fetched, sret, part, sibr, z2m, z2p, z1m, z1p, xr,
+    pv, qv, qhat, hat, fsend, fetched, sret, part, sibr, z2, z1m, z1p, xr,
     exp_c, exp_h, wc, wct, wh, wht, qsum, sel, selt, tabs, qinv, key_ref, kk_ref,
     lsem, ag_s, ag_r, tab_s, tab_r, f_s, f_r, r_s, r_r, rs_s, rs_r,
 ):
@@ -61,7 +72,7 @@
 
     sib, zp, zm, xo = dev(dc=1), dev(dz=1), dev(dz=3), dev(dxh=1)
     partner = [
-        dev(dy=rel // 2, dxl=rel % 2, dxh=(rel % 2) & (rel // 2 % 2)) for rel in range(8)
+        dev(dy=rel // 2, dxl=rel % 2, dxh=flips(rel)) for rel in range(8)
     ]
 
     barrier = pltpu.get_barrier_semaphore()
@@ -84,9 +95,10 @@
     ag = {}
 
     def row(dz, dc, dxh):
-        return dz * CH + dc * 2 * PB + dxh * PB
-
-    def add_ag(name, src, dst, d, parts=(0, 1)):
+        chunk, side = (1 + dxh, dz // 2) if dz % 2 else (dz // 2 * 3, dxh)
+        return chunk * CH + dc * 2 * PB + side * PB
+
+    def add_ag(name, src, dst, d, parts=ALL_PARTS):
         for cq in parts:
             i = len(ag)
             ag[name, cq] = remote(
@@ -105,24 +117,21 @@
     for dxh in range(2):
         add_ag(f"s3{dxh}", row(3, 0, dxh), row(3, 1, dxh), sib)
         add_ag(f"s1{dxh}", row(1, 0, dxh), row(1, 1, dxh), sib)
-        add_ag(f"t{dxh}", row(3, 0, dxh), row(2, 0, dxh), zp, (0,))
-        add_ag(f"t{dxh}", row(1, 0, dxh), row(2, 0, dxh), zm, (1,))
+        add_ag(f"t{dxh}", row(3, 0, dxh), row(2, 0, dxh), zp, ALL_PARTS[:HALF])
+        add_ag(f"t{dxh}", row(1, 0, dxh), row(2, 0, dxh), zm, ALL_PARTS[HALF:])
         add_ag(f"s2{dxh}", row(2, 0, dxh), row(2, 1, dxh), sib)
 
     fetch, back = {}, {}
-    for step, (j, cq) in enumerate(FWD_STEPS):
+    for step, (j, cq) in enumerate(BWD_STEPS):
         for rel in range(1, 8):
-            to = inv_rel(rel)
+            to, theirs = inv_rel(rel), seen_by(rel, j)
             fetch[j, cq, rel] = remote(
                 fsend.at[pl.ds(j * SL + rel * 16, 16), cols(cq)],
-                fetched.at[pl.ds(j * SL + to * 16, 16), cols(cq)],
+                fetched.at[pl.ds(theirs * SL + to * 16, 16), cols(cq)],
                 f_s.at[step, rel], f_r.at[step, to], partner[rel],
             )
-    for step, (j, cq) in enumerate(BWD_STEPS):
-        for rel in range(1, 8):
-            to = inv_rel(rel)
             back[j, cq, rel] = remote(
-                fsend.at[pl.ds(j * SL + rel * 16, 16), cols(cq)],
+                fsend.at[pl.ds(theirs * SL + rel * 16, 16), cols(cq)],
                 sret.at[pl.ds(j * SL + to * 16, 16), cols(cq)],
                 r_s.at[step, rel], r_r.at[step, to], partner[rel],
             )
@@ -138,11 +147,19 @@
             ("sib", j, cq),
             part.at[pl.ds(j * CH + SL, SL), cols(cq)], sibr.at[pl.ds(j * SL, SL), cols(cq)], sib,
         )
-    add_rs(("z", 2, 0), part.at[pl.ds(2 * CH, SL), cols(0)], z2m, zp)
-    add_rs(("z", 2, 1), part.at[pl.ds(2 * CH, SL), cols(1)], z2p, zm)
-    for cq in range(PARTS):
-        add_rs(("z", 1, cq), part.at[pl.ds(CH, SL), cols(cq)], z1m.at[:, cols(cq)], zp)
-        add_rs(("z", 3, cq), part.at[pl.ds(3 * CH, SL), cols(cq)], z1p.at[:, cols(cq)], zm)
+    for cq in ALL_PARTS:
+        add_rs(
+            ("z", 3, cq),
+            part.at[pl.ds(3 * CH, SL), cols(cq)], z2.at[:, cols(cq)], zp if cq < HALF else zm,
+        )
+        for j in (2, 1):
+            there = pl.ds((j - 1) * PB, PB)
+            add_rs(
+                ("zp", j, cq), part.at[pl.ds(j * CH, PB), cols(cq)], z1m.at[there, cols(cq)], zp
+            )
+            add_rs(
+                ("zm", j, cq), part.at[pl.ds(j * CH + PB, PB), cols(cq)], z1p.at[there, cols(cq)], zm
+            )
         add_rs(("x", cq), part.at[pl.ds(PB, PB), cols(cq)], xr.at[:, cols(cq)], xo)
 
     load_p.wait()
@@ -150,19 +167,31 @@
     pinv = 1.0 / jnp.sqrt(jnp.sum(raw * raw, axis=1, keepdims=True) + EPS)
     hat[pl.ds(own, PB), :] = (raw * pinv).astype(BF16)
     pl.semaphore_wait(barrier, 11)
-    for cq in range(PARTS):
+
+    def own_send(cq):
         for name in ("x", "m0", "p0", "s00"):
+            if cq >= 2:
+                ag[name, cq - 2].wait_send()
+                gone.add((name, cq - 2))
             ag[name, cq].start()
+
+    gone = set()
+    own_send(0)
 
     ids = ids_ref[...]
     owner = lax.shift_right_logical(ids, 6)
     ob, og = lax.shift_right_logical(owner, 3), owner & 7
     rel_g = ((lax.shift_right_logical(og, 1) - y) & 3) * 2 + ((og & 1) ^ xl)
-    rel_b = (
-        ((lax.shift_right_logical(ob, 1) - z) & 3) * 4
-        + ((ob & 1) ^ core) * 2
-        + (lax.shift_right_logical(ob, 3) ^ xh)
-    )
+
+    def place(block):
+        dz = (lax.shift_right_logical(block, 1) - z) & 3
+        dxh = lax.shift_right_logical(block, 3) ^ xh
+        odd, far = (dz & 1) == 1, lax.shift_right_logical(dz, 1)
+        chunk, side = jnp.where(odd, 1 + dxh, 3 * far), jnp.where(odd, far, dxh)
+        return chunk, ((block & 1) ^ core) * 2 + side
+
+    chunk, o = place(ob)
+    rel_b = chunk * 4 + o
     keys = (rel_g * 16 + rel_b) * 64 + (ids & 63)
     key_ref[...] = keys
     count = jnp.zeros((128, 128), F32)
@@ -208,10 +237,11 @@
         who, o, slot = lane >> 4, (lane >> 2) & 3, lane & 3
         back_rel = ((4 - (who >> 1)) & 3) * 2 + (who & 1)
         flip = (who & 1) & ((who >> 1) & 1)
-        offset = (o >> 1) * 128 + ((o & 1) ^ flip) * 64
         diag = iota((64, 128), 0) == (who * 8 + slot)[:64]
         for j in range(4):
-            pick = onehot(iota((128, 128), 0) == back_rel * 16 + j * 4 + o)
+            theirs = jnp.where(flip == 1, (0, 2, 1, 3)[j], j)
+            offset = (o >> 1) * 128 + ((o & 1) ^ (flip if j in (0, 3) else 0)) * 64
+            pick = onehot(iota((128, 128), 0) == back_rel * 16 + theirs * 4 + o)
             local = jnp.sum(jnp.where(diag, dot(everything, pick), 0.0), axis=0, keepdims=True)
             target = jnp.where(local >= 0.0, local + offset[:1].astype(F32), -1.0)
             match = jnp.where(iota((CH, SL), 0).astype(F32) == target, 1.0, 0.0)
@@ -266,81 +296,67 @@
 
     positives = ids[:, HARD : HARD + 1]
     pb = lax.shift_right_logical(positives, 6)
-    kk_ref[...] = (
-        ((lax.shift_right_logical(pb, 1) - z) & 3) * CH
-        + ((pb & 1) ^ core) * 128
-        + (lax.shift_right_logical(pb, 3) ^ xh) * 64
-        + (positives & 63)
-    )
-
-    def relay_x(cq):
-        ag["x", cq].wait_recv()
-        for name in ("s01", "m1", "p1"):
-            ag[name, cq].start()
-
-    def relay_z(dxh, cq):
-        ag[f"m{dxh}", cq].wait_recv()
-        ag[f"s3{dxh}", cq].start()
-        if cq == 0:
-            ag[f"t{dxh}", 0].start()
-        ag[f"p{dxh}", cq].wait_recv()
-        ag[f"s1{dxh}", cq].start()
-        if cq == 1:
-            ag[f"t{dxh}", 1].start()
-
-    def relay_two(dxh, cq):
-        ag[f"t{dxh}", cq].wait_recv()
-        ag[f"s2{dxh}", cq].start()
-
-    def from_sib(j, cq):
-        for dxh in range(2):
-            ag[f"s{j}{dxh}", cq].wait_recv()
-
+    chunk, o = place(pb)
+    kk_ref[...] = chunk * CH + o * PB + (positives & 63)
+
+    def sib_relay(cq, *names):
+        for came, sent in names:
+            ag[came, cq].wait_recv()
+            ag[sent, cq].start()
+
+    def z_relay(dxh, cq):
+        ag[f"t{dxh}", cq].start()
+
+    def from_sib(cq, *names):
+        for name in names:
+            ag[name, cq].wait_recv()
+
+    own_send(1)
+    norm_queries(0, 4)
     for copy in ask:
         copy.wait_recv()
     build_selection()
-    norm_queries(0, 6)
-    relay_x(0)
-    relay_z(0, 0)
-    from_sib(0, 0)
-    select(0, 0)
-    norm_queries(6, 16)
-    relay_x(1)
-    relay_z(0, 1)
-    from_sib(0, 1)
-    select(0, 1)
-    cycle_scores(0)
-    relay_z(1, 0)
-    from_sib(1, 0)
-    select(1, 0)
-    from_sib(3, 0)
-    select(3, 0)
-    relay_two(0, 0)
-    relay_two(0, 1)
-    relay_z(1, 1)
-    from_sib(1, 1)
-    select(1, 1)
-    from_sib(3, 1)
-    select(3, 1)
-    cycle_scores(1)
-    relay_two(1, 0)
-    relay_two(1, 1)
-    from_sib(2, 0)
-    select(2, 0)
-    from_sib(2, 1)
-    select(2, 1)
+    for cq in ALL_PARTS:
+        sib_relay(cq, ("x", "s01"), ("m0", "s30"), ("p0", "s10"))
+        if cq + 2 < PARTS:
+            own_send(cq + 2)
+        if cq > 0:
+            ag["m1", cq - 1].start()
+            ag["p1", cq - 1].start()
+        norm_queries(4 + 3 * cq, 7 + 3 * cq)
+        from_sib(cq, "s00", "s01")
+        select(0, cq)
+        from_sib(cq, "s30", "s10")
+        select(1, cq)
+    ag["m1", PARTS - 1].start()
+    ag["p1", PARTS - 1].start()
+    for cq in ALL_PARTS:
+        z_relay(0, cq)
+    for cq in ALL_PARTS:
+        sib_relay(cq, ("m1", "s31"), ("p1", "s11"))
+        z_relay(1, cq)
+        if cq < 2:
+            cycle_scores(cq)
+        from_sib(cq, "s31", "s11")
+        select(2, cq)
+    for cq in ALL_PARTS:
+        sib_relay(cq, ("t0", "s20"), ("t1", "s21"))
+        if cq == 0:
+            cycle_scores(2)
+        from_sib(cq, "s20", "s21")
+        select(3, cq)
     cycle_scores(3)
-    cycle_scores(2)
     build_mask()
 
     pos_score = totals["pos"]
     pos_exp = jnp.exp(pos_score)
     hard_total = pos_exp
-    for j in (0, 1, 3, 2):
-        for cq in range(PARTS):
-            for rel in range(1, 8):
-                fetch[j, cq, rel].wait_recv()
-        at = pl.ds(j * SL, SL)
+    for step in ((0, 1, 2), (3,)):
+        for j in step:
+            for cq in ALL_PARTS:
+                for rel in range(1, 8):
+                    fetch[j, cq, rel].wait_recv()
+        at = pl.ds(step[0] * SL, len(step) * SL)
         scores = SCALE * lax.dot_general(
             qhat[...], fetched[at, :], NT, preferred_element_type=F32
         )
@@ -351,30 +367,45 @@
         copy.wait_send()
     hard_inv = 1.0 / hard_total
 
-    def back_step(j, cq):
+    def back_sums(j):
+        weights = exp_h[:, pl.ds(j * SL, SL)] * hard_inv
+        wh[:, pl.ds(j * SL, SL)] = weights.astype(BF16)
+        wht[pl.ds(j * SL, SL), :] = jnp.transpose(weights).astype(BF16)
+
         def tile(n, carry):
-            at = pl.ds(pl.multiple_of(cq * PW + n * TN, TN), TN)
+            at = pl.ds(pl.multiple_of(n * TN, TN), TN)
             rows = (SCALE * dot(wht[pl.ds(j * SL, SL), :], qhat[:, at])).astype(BF16)
             fsend[pl.ds(j * SL, SL), at] = rows
             sret[pl.ds(j * SL, 16), at] = rows[:16]
             return carry
 
-        lax.fori_loop(0, PW // TN, tile, 0)
+        lax.fori_loop(0, D // TN, tile, 0)
+
+    left = set()
+
+    def back_start(step):
+        j, cq = BWD_STEPS[step]
         for rel in range(1, 8):
+            if step >= DEPTH:
+                earlier = BWD_STEPS[step - DEPTH] + (rel,)
+                back[earlier].wait_send()
+                left.add(earlier)
             back[j, cq, rel].start()
 
-    for j in (2, 1, 3, 0):
-        weights = exp_h[:, pl.ds(j * SL, SL)] * hard_inv
-        wh[:, pl.ds(j * SL, SL)] = weights.astype(BF16)
-        wht[pl.ds(j * SL, SL), :] = jnp.transpose(weights).astype(BF16)
-    for j, cq in BWD_STEPS:
-        back_step(j, cq)
+    back_sums(3)
+    for step in range(DEPTH):
+        back_start(step)
+    for j in (2, 1, 0):
+        back_sums(j)
 
     cycle_total = totals["cycle"]
-    out_l[...] = jnp.log(cycle_total) + jnp.log(hard_total) - 2.0 * pos_score
+    losses = jnp.log(cycle_total) + jnp.log(hard_total) - 2.0 * pos_score
+    for i in range(Q // 128):
+        spread = jnp.broadcast_to(losses[i * 128 : (i + 1) * 128], (128, 128))
+        out_l[pl.ds(i, 1), :] = jnp.transpose(spread)[:1]
     cycle_inv = 1.0 / cycle_total
     correction = 2.0 - pos_exp * hard_inv
-    for j in (2, 1, 3, 0):
+    for j in (3, 2, 1, 0):
         at = pl.ds(j * CH, CH)
         positive = kk_ref[...] == iota((Q, CH), 1) + j * CH
         weights = exp_c[:, at] * cycle_inv - jnp.where(positive, correction, 0.0)
@@ -429,52 +460,62 @@
         mine = pl.ds(j * CH, SL)
         rs["sib", j, cq].wait_recv()
         total = part[mine, at].astype(F32) + sibr[pl.ds(j * SL, SL), at].astype(F32)
-        if (j, cq) == (1, 0):
-            rs["z", 2, 0].wait_recv()
-            total = total + z2m[...].astype(F32)
-        if (j, cq) == (3, 1):
-            rs["z", 2, 1].wait_recv()
-            total = total + z2p[...].astype(F32)
-        if j == 0:
-            rs["z", 1, cq].wait_recv()
-            rs["z", 3, cq].wait_recv()
-            total = total + z1m[:, at].astype(F32) + z1p[:, at].astype(F32)
-        part[mine, at] = total.astype(BF16)
-        if j == 0:
-            rs["x", cq].start()
+        if j == 3:
+            part[mine, at] = total.astype(BF16)
+            rs["z", 3, cq].start()
+        elif j > 0:
+            here = pl.ds((j - 1) * PB, PB)
+            rs["z", 3, cq].wait_recv() if j == 2 else None
+            more = z2[here, at].astype(F32)
+            first, second = total[:PB], total[PB:]
+            if cq < HALF:
+                first = first + more
+            else:
+                second = second + more
+            part[pl.ds(j * CH, PB), at] = first.astype(BF16)
+            rs["zp", j, cq].start()
+            part[pl.ds(j * CH + PB, PB), at] = second.astype(BF16)
+            rs["zm", j, cq].start()
         else:
-            rs["z", j, cq].start()
-
-    query_rows(0)
-    partial(2, 0)
-    partial(2, 1)
-    reduce(2, 0)
-    reduce(2, 1)
-    query_rows(1)
-    partial(1, 0)
-    partial(3, 0)
-    reduce(1, 0)
-    reduce(3, 0)
-    query_rows(2)
-    partial(1, 1)
-    partial(3, 1)
-    reduce(1, 1)
-    reduce(3, 1)
-    query_rows(3)
-    partial(0, 0)
-    partial(0, 1)
-    reduce(0, 0)
-    reduce(0, 1)
+            for dxh in (1, 0):
+                rs["zp", 1 + dxh, cq].wait_recv()
+                rs["zm", 1 + dxh, cq].wait_recv()
+                here = pl.ds(dxh * PB, PB)
+                both = z1m[here, at].astype(F32) + z1p[here, at].astype(F32)
+                both = both + total[dxh * PB : (dxh + 1) * PB]
+                if dxh == 1:
+                    part[here, at] = both.astype(BF16)
+                    rs["x", cq].start()
+                else:
+                    qsum[:PB, at] = both
+
+    waiting = []
+    for step, (j, cq) in enumerate(BWD_STEPS):
+        partial(j, cq)
+        if step + DEPTH < STEPS:
+            back_start(step + DEPTH)
+        waiting.append((j, cq))
+        if len(waiting) > 1:
+            reduce(*waiting.pop(0))
+        if step % 2 == 1 and step // 2 < Q // QR:
+            query_rows(step // 2)
+    reduce(*waiting.pop(0))
 
     unit = pv[...].astype(F32) * pinv
-    for cq in range(PARTS):
+    for cq in ALL_PARTS:
         rs["x", cq].wait_recv()
-    total = part[pl.ds(0, PB), :].astype(F32) + xr[...].astype(F32)
+    total = qsum[:PB, :] + xr[...].astype(F32)
     along = jnp.sum(unit * total, axis=1, keepdims=True)
     out_p[...] = ((total - unit * along) * pinv).astype(BF16)
 
-    for copy in ask + list(ag.values()) + list(back.values()) + list(rs.values()):
+    for key, copy in ag.items():
+        if key not in gone:
+            copy.wait_send()
+    for copy in ask + list(rs.values()):
         copy.wait_send()
+    for key, copy in back.items():
+        if key not in left:
+            copy.wait_send()
     for copy in store_q:
         copy.wait()
 
@@ -489,7 +530,7 @@
         out_shape=(
             jax.ShapeDtypeStruct((Q, D), BF16),
             jax.ShapeDtypeStruct((PB, D), BF16),
-            jax.ShapeDtypeStruct((Q, 1), F32),
+            jax.ShapeDtypeStruct((Q // 128, 128), F32),
         ),
         in_specs=[any_spec, any_spec, vmem_spec],
         out_specs=(any_spec, vmem_spec, vmem_spec),
@@ -503,8 +544,7 @@
             pltpu.VMEM((4 * SL, D), BF16),
             pltpu.VMEM((4 * CH, D), BF16),
             pltpu.VMEM((4 * SL, D), BF16),
-            pltpu.VMEM((SL, PW), BF16),
-            pltpu.VMEM((SL, PW), BF16),
+            pltpu.VMEM((SL, D), BF16),
             pltpu.VMEM((SL, D), BF16),
             pltpu.VMEM((SL, D), BF16),
             pltpu.VMEM((PB, D), BF16),
@@ -522,11 +562,11 @@
             pltpu.VMEM((Q, HARD + 1), jnp.int32),
             pltpu.VMEM((Q, 1), jnp.int32),
             dma((8,)),
-            dma((32,)), dma((32,)),
+            dma((15 * PARTS,)), dma((15 * PARTS,)),
             dma((8,)), dma((8,)),
-            dma((8, 8)), dma((8, 8)),
-            dma((8, 8)), dma((8, 8)),
-            dma((16,)), dma((16,)),
+            dma((STEPS, 8)), dma((STEPS, 8)),
+            dma((STEPS, 8)), dma((STEPS, 8)),
+            dma((10 * PARTS,)), dma((10 * PARTS,)),
         ],
         compiler_params=pltpu.CompilerParams(
             collective_id=0, has_side_effects=True, vmem_limit_bytes=63 * 2**20

time: 170 us -> 150 us (0.88)
  Pallas kernels: 160 us -> 141 us
    pallas_call x1, Pallas kernels: 160 us -> 141 us  [shards(): pl.pallas_call(kernel, out_shape=(jax.ShapeDtypeStruct((Q, D), BF16), jax...]
    unnamed x4 -> x7, local copies, waits for them, and re-layouts: 5.55 us -> 6.13 us
where the time goes in v2:
time: 150 us
  Pallas kernels  141 us (94%)
  local copies, waits for them, and re-layouts  6.99 us (5%)
    pallas_call x1, Pallas kernels, shards(): pl.pallas_call(kernel, out_shape=(jax.ShapeDtypeStruct((Q, D), BF16), jax...  141 us
    unnamed x7, local copies, waits for them, and re-layouts  6.13 us

profile of v2, /device:TPU:1, one launch (start us, length us, event | category | flops | bytes accessed | tf_op | source)
XLA Modules:
  0.0 149.9 jit_solution(16336220091043997963)
XLA Ops:
  0.6 0.7 pad_add_fusion
  1.4 0.9 copy.10.ids_ref
  2.2 141.5 %shard_map.67 = (bf16[512,4096]{1,0:T(8,128)(2,1)}, bf16[64,4096]{1,0:T(8,128)(2,1)}, f32[4,128]{1,0:T(4,128)}) custom-call(bf16[64,4096]{1,0:T(8,128)(2,1)} %passages.1, bf16[512,4096]{1,0:T(8,128)(2,1)} %queries.1, s32[512,9]{1,0:T(8,128)} %copy.10.ids_ref), custom_call_target="tpu_custom_call" | custom-call | flops 19327352832 | bytes 8388608 | tf_op jit(solution)/shard_map/pallas_call | solution.py:528
  143.7 0.0 copy-start
  143.7 0.0 copy-start.1
  143.7 4.8 %copy.14 = bf16[512,4096]{1,0:T(8,128)(2,1)} copy(bf16[512,4096]{1,0:T(8,128)(2,1)} %get-tuple-element.12) | data formatting | bytes 8388608
  148.5 0.0 copy-done
  148.5 0.8 copy.15
  149.3 0.0 copy-done.1
  149.3 0.6 copy.16
Async XLA Ops:
  143.7 4.8 %copy-start = (bf16[64,4096]{1,0:T(8,128)(2,1)S(1)}, bf16[64,4096]{1,0:T(8,128)(2,1)}, u32[]{:S(2)}) copy-start(bf16[64,4096]{1,0:T(8,128)(2,1)} %get-tuple-element.13) | copy-start | bytes 1572868
  143.7 5.6 %copy-start.1 = (f32[4,128]{1,0:T(4,128)S(1)}, f32[4,128]{1,0:T(4,128)}, u32[]{:S(2)}) copy-start(f32[4,128]{1,0:T(4,128)} %get-tuple-element.8) | copy-start | bytes 6148

commit v3 on v2

--- a/solution.py
+++ b/solution.py
@@ -19,7 +19,7 @@
 TN = 512
 HALF = PARTS // 2
 ALL_PARTS = tuple(range(PARTS))
-DEPTH = 3
+DEPTH = 6
 STEPS = 4 * PARTS
 BWD_STEPS = tuple((j, cq) for j in (3, 2, 1, 0) for cq in ALL_PARTS)
 MESH = pl.DeviceIdType.MESH
@@ -54,7 +54,7 @@
 
 
 def kernel(
-    passages, queries, ids_ref, out_q, out_p, out_l,
+    passages, queries, ids_ref, pos_ref, out_q, out_p, out_l,
     pv, qv, qhat, hat, fsend, fetched, sret, part, sibr, z2, z1m, z1p, xr,
     exp_c, exp_h, wc, wct, wh, wht, qsum, sel, selt, tabs, qinv, key_ref, kk_ref,
     lsem, ag_s, ag_r, tab_s, tab_r, f_s, f_r, r_s, r_r, rs_s, rs_r,
@@ -162,27 +162,6 @@
             )
         add_rs(("x", cq), part.at[pl.ds(PB, PB), cols(cq)], xr.at[:, cols(cq)], xo)
 
-    load_p.wait()
-    raw = pv[...].astype(F32)
-    pinv = 1.0 / jnp.sqrt(jnp.sum(raw * raw, axis=1, keepdims=True) + EPS)
-    hat[pl.ds(own, PB), :] = (raw * pinv).astype(BF16)
-    pl.semaphore_wait(barrier, 11)
-
-    def own_send(cq):
-        for name in ("x", "m0", "p0", "s00"):
-            if cq >= 2:
-                ag[name, cq - 2].wait_send()
-                gone.add((name, cq - 2))
-            ag[name, cq].start()
-
-    gone = set()
-    own_send(0)
-
-    ids = ids_ref[...]
-    owner = lax.shift_right_logical(ids, 6)
-    ob, og = lax.shift_right_logical(owner, 3), owner & 7
-    rel_g = ((lax.shift_right_logical(og, 1) - y) & 3) * 2 + ((og & 1) ^ xl)
-
     def place(block):
         dz = (lax.shift_right_logical(block, 1) - z) & 3
         dxh = lax.shift_right_logical(block, 3) ^ xh
@@ -190,17 +169,19 @@
         chunk, side = jnp.where(odd, 1 + dxh, 3 * far), jnp.where(odd, far, dxh)
         return chunk, ((block & 1) ^ core) * 2 + side
 
-    chunk, o = place(ob)
-    rel_b = chunk * 4 + o
-    keys = (rel_g * 16 + rel_b) * 64 + (ids & 63)
-    key_ref[...] = keys
+    ids = ids_ref[...]
+    owner = lax.shift_right_logical(ids, 6)
+    og = owner & 7
+    rel_g = ((lax.shift_right_logical(og, 1) - y) & 3) * 2 + ((og & 1) ^ xl)
+    chunk, o = place(lax.shift_right_logical(owner, 3))
+    keys = (rel_g * 16 + chunk * 4 + o) * 64 + (ids & 63)
     count = jnp.zeros((128, 128), F32)
-    lane_q = iota((Q, 128), 1)
+    sub_q = iota((128, Q), 0)
     for h in range(HARD):
-        column = keys[:, h : h + 1]
-        hi = onehot(lax.shift_right_logical(column, 6) == lane_q)
-        lo = onehot((column & 63) == lane_q)
-        count = count + lax.dot_general(lo, hi, TN_DIMS, preferred_element_type=F32)
+        key = keys[h : h + 1]
+        hi = onehot(lax.shift_right_logical(key, 6) == sub_q)
+        lo = onehot((key & 63) == sub_q)
+        count = count + lax.dot_general(lo, hi, NT, preferred_element_type=F32)
     present = count > 0.5
     sub = iota((128, 128), 0)
     rank = dot(onehot(iota((128, 128), 1) < sub), onehot(present))
@@ -212,6 +193,23 @@
         found = jnp.sum(hit, axis=0, keepdims=True) - 1.0
         table = jnp.where(iota((8, 128), 0) == slot, found, table)
     tabs[0] = table
+
+    load_p.wait()
+    raw = pv[...].astype(F32)
+    pinv = 1.0 / jnp.sqrt(jnp.sum(raw * raw, axis=1, keepdims=True) + EPS)
+    hat[pl.ds(own, PB), :] = (raw * pinv).astype(BF16)
+    pl.semaphore_wait(barrier, 11)
+
+    def own_send(cq):
+        for name in ("x", "m0", "p0", "s00"):
+            if cq >= 2:
+                ag[name, cq - 2].wait_send()
+                gone.add((name, cq - 2))
+            ag[name, cq].start()
+
+    gone = set()
+    own_send(0)
+
     ask = []
     for rel in range(1, 8):
         to = inv_rel(rel)
@@ -294,10 +292,15 @@
             jnp.where(positive, scores, 0.0), axis=1, keepdims=True
         )
 
-    positives = ids[:, HARD : HARD + 1]
-    pb = lax.shift_right_logical(positives, 6)
-    chunk, o = place(pb)
-    kk_ref[...] = chunk * CH + o * PB + (positives & 63)
+    positives = pos_ref[...]
+    chunk, o = place(lax.shift_right_logical(positives, 6))
+    spots = chunk * CH + o * PB + (positives & 63)
+    stacked = jnp.concatenate(
+        [keys.astype(F32), jnp.broadcast_to(spots.astype(F32), (120, Q))], axis=0
+    )
+    turned = jnp.transpose(stacked).astype(jnp.int32)
+    key_ref[...] = turned
+    kk_ref[...] = turned[:, HARD : HARD + 1]
 
     def sib_relay(cq, *names):
         for came, sent in names:
@@ -367,19 +370,24 @@
         copy.wait_send()
     hard_inv = 1.0 / hard_total
 
-    def back_sums(j):
-        weights = exp_h[:, pl.ds(j * SL, SL)] * hard_inv
-        wh[:, pl.ds(j * SL, SL)] = weights.astype(BF16)
-        wht[pl.ds(j * SL, SL), :] = jnp.transpose(weights).astype(BF16)
+    def back_sums(first, chunks, parts=ALL_PARTS):
+        slots = pl.ds(first * SL, chunks * SL)
 
         def tile(n, carry):
             at = pl.ds(pl.multiple_of(n * TN, TN), TN)
-            rows = (SCALE * dot(wht[pl.ds(j * SL, SL), :], qhat[:, at])).astype(BF16)
-            fsend[pl.ds(j * SL, SL), at] = rows
-            sret[pl.ds(j * SL, 16), at] = rows[:16]
+            rows = (SCALE * dot(wht[slots, :], qhat[:, at])).astype(BF16)
+            fsend[slots, at] = rows
+            for i in range(chunks):
+                sret[pl.ds((first + i) * SL, 16), at] = rows[i * SL : i * SL + 16]
             return carry
 
-        lax.fori_loop(0, D // TN, tile, 0)
+        lax.fori_loop(parts[0] * PW // TN, (parts[-1] + 1) * PW // TN, tile, 0)
+
+    def hard_weights(first, chunks):
+        slots = pl.ds(first * SL, chunks * SL)
+        weights = exp_h[:, slots] * hard_inv
+        wh[:, slots] = weights.astype(BF16)
+        wht[slots, :] = jnp.transpose(weights).astype(BF16)
 
     left = set()
 
@@ -392,11 +400,15 @@
                 left.add(earlier)
             back[j, cq, rel].start()
 
-    back_sums(3)
-    for step in range(DEPTH):
+    hard_weights(3, 1)
+    back_sums(3, 1, ALL_PARTS[:1])
+    back_start(0)
+    back_sums(3, 1, ALL_PARTS[1:])
+    back_start(1)
+    hard_weights(0, 3)
+    back_sums(0, 3)
+    for step in range(2, DEPTH):
         back_start(step)
-    for j in (2, 1, 0):
-        back_sums(j)
 
     cycle_total = totals["cycle"]
     losses = jnp.log(cycle_total) + jnp.log(hard_total) - 2.0 * pos_score
@@ -412,10 +424,11 @@
         wc[:, at] = weights.astype(BF16)
         wct[at, :] = jnp.transpose(weights).astype(BF16)
 
-    QR = 128
+    QR = 256
     store_q = []
-
-    def query_rows(block):
+    along_q = {}
+
+    def query_tiles(block, first, last):
         rows = pl.ds(block * QR, QR)
         inverse = qinv[rows, 0:1]
 
@@ -426,7 +439,13 @@
             unit = qv[rows, at].astype(F32) * inverse
             return total + jnp.sum(unit * tile, axis=1, keepdims=True)
 
-        along = lax.fori_loop(0, D // TN, product, jnp.zeros((QR, 1), F32))
+        start = along_q.get(block, jnp.zeros((QR, 1), F32))
+        along_q[block] = lax.fori_loop(first, last, product, start)
+
+    def query_store(block):
+        rows = pl.ds(block * QR, QR)
+        inverse = qinv[rows, 0:1]
+        along = along_q[block]
 
         def project(n, carry):
             at = pl.ds(pl.multiple_of(n * TN, TN), TN)
@@ -439,6 +458,13 @@
             pltpu.make_async_copy(qv.at[rows, :], out_q.at[rows, :], lsem.at[2 + block])
         )
         store_q[-1].start()
+
+    def query_work(i):
+        block, piece = i // 3, i % 3
+        if piece < 2:
+            query_tiles(block, piece * 4, piece * 4 + 4)
+        else:
+            query_store(block)
 
     def partial(j, cq):
         for rel in range(1, 8):
@@ -497,8 +523,8 @@
         waiting.append((j, cq))
         if len(waiting) > 1:
             reduce(*waiting.pop(0))
-        if step % 2 == 1 and step // 2 < Q // QR:
-            query_rows(step // 2)
+        if 1 <= step <= 6:
+            query_work(step - 1)
     reduce(*waiting.pop(0))
 
     unit = pv[...].astype(F32) * pinv
@@ -520,8 +546,25 @@
         copy.wait()
 
 
+def hand_over(in_q, in_p, in_l, out_q, out_p, out_l, hold_q, hold_p, hold_l, sem_in, sem_out):
+    pieces = [(in_p, hold_p, out_p), (in_l, hold_l, out_l)]
+    for i in range(8):
+        rows = pl.ds(i * (Q // 8), Q // 8)
+        pieces.append((in_q.at[rows, :], hold_q.at[rows, :], out_q.at[rows, :]))
+    loads, stores = [], []
+    for i, (source, hold, target) in enumerate(pieces):
+        loads.append(pltpu.make_async_copy(source, hold, sem_in.at[i]))
+        stores.append(pltpu.make_async_copy(hold, target, sem_out.at[i]))
+    for load in loads:
+        load.start()
+    for load, store in zip(loads, stores):
+        load.wait()
+        store.start()
+    for store in stores:
+        store.wait()
+
+
 def shards(queries, passages, positives, hard_ids):
-    ids = jnp.concatenate([hard_ids, positives[:, None]], axis=1)
     dma = pltpu.SemaphoreType.DMA
     any_spec = pl.BlockSpec(memory_space=pl.ANY)
     vmem_spec = pl.BlockSpec(memory_space=pltpu.VMEM)
@@ -532,7 +575,7 @@
             jax.ShapeDtypeStruct((PB, D), BF16),
             jax.ShapeDtypeStruct((Q // 128, 128), F32),
         ),
-        in_specs=[any_spec, any_spec, vmem_spec],
+        in_specs=[any_spec, any_spec, vmem_spec, vmem_spec],
         out_specs=(any_spec, vmem_spec, vmem_spec),
         scratch_shapes=[
             pltpu.VMEM((PB, D), BF16),
@@ -554,12 +597,12 @@
             pltpu.VMEM((4 * CH, Q), BF16),
             pltpu.VMEM((Q, 4 * SL), BF16),
             pltpu.VMEM((4 * SL, Q), BF16),
-            pltpu.VMEM((128, D), F32),
+            pltpu.VMEM((256, D), F32),
             pltpu.VMEM((4 * SL, CH), BF16),
             pltpu.VMEM((4 * CH, SL), BF16),
             pltpu.VMEM((8, 8, 128), F32),
             pltpu.VMEM((Q, 128), F32),
-            pltpu.VMEM((Q, HARD + 1), jnp.int32),
+            pltpu.VMEM((Q, 128), jnp.int32),
             pltpu.VMEM((Q, 1), jnp.int32),
             dma((8,)),
             dma((15 * PARTS,)), dma((15 * PARTS,)),
@@ -574,7 +617,26 @@
         cost_estimate=pl.CostEstimate(
             flops=6 * Q * 1536 * D, bytes_accessed=4 * Q * D, transcendentals=Q * 1536
         ),
-    )(passages, queries, ids)
+    )(passages, queries, hard_ids.T, positives.reshape(1, Q))
+    query_grads, passage_grads, losses = pl.pallas_call(
+        hand_over,
+        out_shape=(
+            jax.ShapeDtypeStruct((Q, D), BF16),
+            jax.ShapeDtypeStruct((PB, D), BF16),
+            jax.ShapeDtypeStruct((Q // 128, 128), F32),
+        ),
+        in_specs=[any_spec] * 3,
+        out_specs=(any_spec,) * 3,
+        scratch_shapes=[
+            pltpu.VMEM((Q, D), BF16),
+            pltpu.VMEM((PB, D), BF16),
+            pltpu.VMEM((Q // 128, 128), F32),
+            dma((10,)),
+            dma((10,)),
+        ],
+        compiler_params=pltpu.CompilerParams(vmem_limit_bytes=63 * 2**20),
+        cost_estimate=pl.CostEstimate(flops=0, bytes_accessed=4 * Q * D, transcendentals=0),
+    )(query_grads, passage_grads, losses)
     return query_grads, passage_grads, losses.reshape(Q)
 
 

time: 150 us -> 142 us (0.947)
  local copies, waits for them, and re-layouts: 6.99 us -> 0 us
    unnamed x7 -> x0, local copies, waits for them, and re-layouts: 6.13 us -> none
    pallas_call x1, Pallas kernels: 141 us -> 136 us  [shards(): pl.pallas_call(kernel, out_shape=(jax.ShapeDtypeStruct((Q, D), BF16), jax...]
    pallas_call x0 -> x1, Pallas kernels: none -> 4.18 us  [shards(): pl.pallas_call(hand_over, out_shape=(jax.ShapeDtypeStruct((Q, D), BF16),...]
where the time goes in v3:
time: 142 us; the launch traced here: 141 us
  Pallas kernels  141 us (99%)
    pallas_call x1, Pallas kernels, shards(): pl.pallas_call(kernel, out_shape=(jax.ShapeDtypeStruct((Q, D), BF16), jax...  136 us
    pallas_call x1, Pallas kernels, shards(): pl.pallas_call(hand_over, out_shape=(jax.ShapeDtypeStruct((Q, D), BF16),...  4.18 us

profile of v3, /device:TPU:1, one launch (start us, length us, event | category | flops | bytes accessed | tf_op | source)
XLA Modules:
  0.0 141.3 jit_solution(1203291715054966617)
XLA Ops:
  0.6 136.4 %shard_map.67 = (bf16[512,4096]{1,0:T(8,128)(2,1)}, bf16[64,4096]{1,0:T(8,128)(2,1)}, f32[4,128]{1,0:T(4,128)}) custom-call(bf16[64,4096]{1,0:T(8,128)(2,1)} %passages.1, bf16[512,4096]{1,0:T(8,128)(2,1)} %queries.1, s32[8,512]{1,0:T(8,128)} %bitcast.3, s32[1,512]{1,0:T(1,128)} %bitcast.4), custom_call_target="tpu_custom_call" | custom-call | flops 19327352832 | bytes 8388608 | tf_op jit(solution)/shard_map/pallas_call | solution.py:571
  137.0 4.2 %shard_map.68 = (bf16[512,4096]{1,0:T(8,128)(2,1)}, bf16[64,4096]{1,0:T(8,128)(2,1)}, f32[4,128]{1,0:T(4,128)}) custom-call(bf16[512,4096]{1,0:T(8,128)(2,1)} %get-tuple-element.9.in_q, bf16[64,4096]{1,0:T(8,128)(2,1)} %get-tuple-element.10.in_p, f32[4,128]{1,0:T(4,128)} %get-tuple-element.11.in_l), custom_call_target="tpu_custom_call" | custom-call | bytes 8388608 | tf_op jit(solution)/shard_map/pallas_call | solution.py:621

commit v4 on v3

--- a/solution.py
+++ b/solution.py
@@ -19,7 +19,7 @@
 TN = 512
 HALF = PARTS // 2
 ALL_PARTS = tuple(range(PARTS))
-DEPTH = 6
+AHEAD = (4,) * 16
 STEPS = 4 * PARTS
 BWD_STEPS = tuple((j, cq) for j in (3, 2, 1, 0) for cq in ALL_PARTS)
 MESH = pl.DeviceIdType.MESH
@@ -316,36 +316,31 @@
 
     own_send(1)
     norm_queries(0, 4)
+    own_send(2)
     for copy in ask:
         copy.wait_recv()
     build_selection()
+    own_send(3)
     for cq in ALL_PARTS:
         sib_relay(cq, ("x", "s01"), ("m0", "s30"), ("p0", "s10"))
-        if cq + 2 < PARTS:
-            own_send(cq + 2)
-        if cq > 0:
-            ag["m1", cq - 1].start()
-            ag["p1", cq - 1].start()
+        ag["m1", cq].start()
+        ag["p1", cq].start()
+        z_relay(0, cq)
         norm_queries(4 + 3 * cq, 7 + 3 * cq)
         from_sib(cq, "s00", "s01")
         select(0, cq)
         from_sib(cq, "s30", "s10")
         select(1, cq)
-    ag["m1", PARTS - 1].start()
-    ag["p1", PARTS - 1].start()
-    for cq in ALL_PARTS:
-        z_relay(0, cq)
     for cq in ALL_PARTS:
         sib_relay(cq, ("m1", "s31"), ("p1", "s11"))
         z_relay(1, cq)
-        if cq < 2:
-            cycle_scores(cq)
         from_sib(cq, "s31", "s11")
         select(2, cq)
+    for j in range(3):
+        cycle_scores(j)
     for cq in ALL_PARTS:
         sib_relay(cq, ("t0", "s20"), ("t1", "s21"))
-        if cq == 0:
-            cycle_scores(2)
+    for cq in ALL_PARTS:
         from_sib(cq, "s20", "s21")
         select(3, cq)
     cycle_scores(3)
@@ -354,6 +349,9 @@
     pos_score = totals["pos"]
     pos_exp = jnp.exp(pos_score)
     hard_total = pos_exp
+    for (j, cq, rel), copy in fetch.items():
+        if j != 3:
+            copy.wait_send()
     for step in ((0, 1, 2), (3,)):
         for j in step:
             for cq in ALL_PARTS:
@@ -366,8 +364,9 @@
         raised = exp_h[:, at] * jnp.exp(scores)
         exp_h[:, at] = raised
         hard_total = hard_total + jnp.sum(raised, axis=1, keepdims=True)
-    for copy in fetch.values():
-        copy.wait_send()
+    for (j, cq, rel), copy in fetch.items():
+        if j == 3:
+            copy.wait_send()
     hard_inv = 1.0 / hard_total
 
     def back_sums(first, chunks, parts=ALL_PARTS):
@@ -394,8 +393,8 @@
     def back_start(step):
         j, cq = BWD_STEPS[step]
         for rel in range(1, 8):
-            if step >= DEPTH:
-                earlier = BWD_STEPS[step - DEPTH] + (rel,)
+            earlier = BWD_STEPS[max(step - AHEAD[step], 0)] + (rel,)
+            if step >= AHEAD[step] and earlier not in left:
                 back[earlier].wait_send()
                 left.add(earlier)
             back[j, cq, rel].start()
@@ -407,7 +406,7 @@
     back_start(1)
     hard_weights(0, 3)
     back_sums(0, 3)
-    for step in range(2, DEPTH):
+    for step in range(2, AHEAD[0]):
         back_start(step)
 
     cycle_total = totals["cycle"]
@@ -467,9 +466,6 @@
             query_store(block)
 
     def partial(j, cq):
-        for rel in range(1, 8):
-            back[j, cq, rel].wait_recv()
-
         def tile(n, carry):
             at = pl.ds(pl.multiple_of(cq * PW + n * TN, TN), TN)
             total = SCALE * dot(wct[pl.ds(j * CH, CH), :], qhat[:, at]) + dot(
@@ -515,18 +511,35 @@
                 else:
                     qsum[:PB, at] = both
 
-    waiting = []
+    for key, copy in ag.items():
+        if key not in gone:
+            copy.wait_send()
+    for copy in ask:
+        copy.wait_send()
+    for i in range(3):
+        query_work(i)
+    waiting, started = [], AHEAD[0]
     for step, (j, cq) in enumerate(BWD_STEPS):
+        for rel in range(1, 8):
+            back[j, cq, rel].wait_recv()
+        while started < STEPS and started - AHEAD[started] <= step:
+            back_start(started)
+            started += 1
         partial(j, cq)
-        if step + DEPTH < STEPS:
-            back_start(step + DEPTH)
         waiting.append((j, cq))
-        if len(waiting) > 1:
+        while len(waiting) > (1 if step < 12 else 0):
             reduce(*waiting.pop(0))
-        if 1 <= step <= 6:
-            query_work(step - 1)
-    reduce(*waiting.pop(0))
-
+        if step in (3, 5, 7):
+            query_work(3 + (step - 3) // 2)
+
+    for key, copy in back.items():
+        if key not in left:
+            copy.wait_send()
+    for key, copy in rs.items():
+        if key[0] != "x":
+            copy.wait_send()
+    for copy in store_q:
+        copy.wait()
     unit = pv[...].astype(F32) * pinv
     for cq in ALL_PARTS:
         rs["x", cq].wait_recv()
@@ -534,16 +547,8 @@
     along = jnp.sum(unit * total, axis=1, keepdims=True)
     out_p[...] = ((total - unit * along) * pinv).astype(BF16)
 
-    for key, copy in ag.items():
-        if key not in gone:
-            copy.wait_send()
-    for copy in ask + list(rs.values()):
-        copy.wait_send()
-    for key, copy in back.items():
-        if key not in left:
-            copy.wait_send()
-    for copy in store_q:
-        copy.wait()
+    for cq in ALL_PARTS:
+        rs["x", cq].wait_send()
 
 
 def hand_over(in_q, in_p, in_l, out_q, out_p, out_l, hold_q, hold_p, hold_l, sem_in, sem_out):

time: 142 us -> 140 us (0.986)
  Pallas kernels: 141 us -> 139 us
    pallas_call x1, Pallas kernels: 136 us -> 135 us  [shards(): pl.pallas_call(kernel, out_shape=(jax.ShapeDtypeStruct((Q, D), BF16), jax...]
where the time goes in v4:
time: 140 us
  Pallas kernels  139 us (99%)
    pallas_call x1, Pallas kernels, shards(): pl.pallas_call(kernel, out_shape=(jax.ShapeDtypeStruct((Q, D), BF16), jax...  135 us
    pallas_call x1, Pallas kernels, shards(): pl.pallas_call(hand_over, out_shape=(jax.ShapeDtypeStruct((Q, D), BF16),...  4.18 us

profile of v4, /device:TPU:1, one launch (start us, length us, event | category | flops | bytes accessed | tf_op | source)
XLA Modules:
  0.0 139.8 jit_solution(17892697497459068962)
XLA Ops:
  0.6 134.8 %shard_map.67 = (bf16[512,4096]{1,0:T(8,128)(2,1)}, bf16[64,4096]{1,0:T(8,128)(2,1)}, f32[4,128]{1,0:T(4,128)}) custom-call(bf16[64,4096]{1,0:T(8,128)(2,1)} %passages.1, bf16[512,4096]{1,0:T(8,128)(2,1)} %queries.1, s32[8,512]{1,0:T(8,128)} %bitcast.3, s32[1,512]{1,0:T(1,128)} %bitcast.4), custom_call_target="tpu_custom_call" | custom-call | flops 19327352832 | bytes 8388608 | tf_op jit(solution)/shard_map/pallas_call | solution.py:576
  135.5 4.2 %shard_map.68 = (bf16[512,4096]{1,0:T(8,128)(2,1)}, bf16[64,4096]{1,0:T(8,128)(2,1)}, f32[4,128]{1,0:T(4,128)}) custom-call(bf16[512,4096]{1,0:T(8,128)(2,1)} %get-tuple-element.9.in_q, bf16[64,4096]{1,0:T(8,128)(2,1)} %get-tuple-element.10.in_p, f32[4,128]{1,0:T(4,128)} %get-tuple-element.11.in_l), custom_call_target="tpu_custom_call" | custom-call | bytes 8388608 | tf_op jit(solution)/shard_map/pallas_call | solution.py:626

commit v5 on v4

--- a/solution.py
+++ b/solution.py
@@ -353,14 +353,17 @@
         if j != 3:
             copy.wait_send()
     for step in ((0, 1, 2), (3,)):
-        for j in step:
-            for cq in ALL_PARTS:
-                for rel in range(1, 8):
-                    fetch[j, cq, rel].wait_recv()
         at = pl.ds(step[0] * SL, len(step) * SL)
-        scores = SCALE * lax.dot_general(
-            qhat[...], fetched[at, :], NT, preferred_element_type=F32
-        )
+        scores = jnp.zeros((Q, len(step) * SL), F32)
+        for piece in (ALL_PARTS,) if step[0] == 0 else [(cq,) for cq in ALL_PARTS]:
+            for j in step:
+                for cq in piece:
+                    for rel in range(1, 8):
+                        fetch[j, cq, rel].wait_recv()
+            here = pl.ds(piece[0] * PW, len(piece) * PW)
+            scores = scores + SCALE * lax.dot_general(
+                qhat[:, here], fetched[at, here], NT, preferred_element_type=F32
+            )
         raised = exp_h[:, at] * jnp.exp(scores)
         exp_h[:, at] = raised
         hard_total = hard_total + jnp.sum(raised, axis=1, keepdims=True)

time: 140 us -> 139 us (level)
    pallas_call x1, Pallas kernels: 135 us -> 133 us  [shards(): pl.pallas_call(kernel, out_shape=(jax.ShapeDtypeStruct((Q, D), BF16), jax...]
where the time goes in v5:
time: 139 us; the launch traced here: 138 us
  Pallas kernels  138 us (99%)
    pallas_call x1, Pallas kernels, shards(): pl.pallas_call(kernel, out_shape=(jax.ShapeDtypeStruct((Q, D), BF16), jax...  133 us
    pallas_call x1, Pallas kernels, shards(): pl.pallas_call(hand_over, out_shape=(jax.ShapeDtypeStruct((Q, D), BF16),...  4.18 us

profile of v5, /device:TPU:1, one launch (start us, length us, event | category | flops | bytes accessed | tf_op | source)
XLA Modules:
  0.0 138.4 jit_solution(17939796558835947508)
XLA Ops:
  0.6 133.4 %shard_map.67 = (bf16[512,4096]{1,0:T(8,128)(2,1)}, bf16[64,4096]{1,0:T(8,128)(2,1)}, f32[4,128]{1,0:T(4,128)}) custom-call(bf16[64,4096]{1,0:T(8,128)(2,1)} %passages.1, bf16[512,4096]{1,0:T(8,128)(2,1)} %queries.1, s32[8,512]{1,0:T(8,128)} %bitcast.3, s32[1,512]{1,0:T(1,128)} %bitcast.4), custom_call_target="tpu_custom_call" | custom-call | flops 19327352832 | bytes 8388608 | tf_op jit(solution)/shard_map/pallas_call | solution.py:579
  134.1 4.2 %shard_map.68 = (bf16[512,4096]{1,0:T(8,128)(2,1)}, bf16[64,4096]{1,0:T(8,128)(2,1)}, f32[4,128]{1,0:T(4,128)}) custom-call(bf16[512,4096]{1,0:T(8,128)(2,1)} %get-tuple-element.9.in_q, bf16[64,4096]{1,0:T(8,128)(2,1)} %get-tuple-element.10.in_p, f32[4,128]{1,0:T(4,128)} %get-tuple-element.11.in_l), custom_call_target="tpu_custom_call" | custom-call | bytes 8388608 | tf_op jit(solution)/shard_map/pallas_call | solution.py:629
